TPU v7x, 512 devices: a whole 4x4x16 slice. The times are simulated.
512 devices in a mesh: ctx: 64 (over y, z), mp: 8 (over x, core).
Axes of the slice: x: 4, y: 4, z: 16, core: 2. Of those that a mesh axis runs over, the one named last changes fastest.
Arguments:
- residual: bfloat16 [16384, 2048], P('ctx', 'mp'), may hold values from -6 to 6
- delta_query: bfloat16 [16384, 2048], P('ctx', 'mp'), may hold values from -6 to 6
- delta_key: bfloat16 [16384, 2048], P('ctx', 'mp'), may hold values from -6 to 6
- delta_value: bfloat16 [16384, 4096], P('ctx', 'mp'), may hold values from -6 to 6
- write_strength: float32 [32, 16384], P('mp', 'ctx'), may hold values from 0.05 to 0.9
- log_decay: float32 [32, 16384], P('mp', 'ctx'), may hold values from -1 to 0
- output_gate: bfloat16 [16384, 4096], P('ctx', 'mp'), may hold values from -6 to 6
- norm_gain: float32 [128], replicated, may hold values from 0.1 to 1.9
- attn_query: bfloat16 [16384, 4096], P('ctx', 'mp'), may hold values from -9 to 9
- attn_key: bfloat16 [16384, 512], P('ctx'), may hold values from -9 to 9
- attn_value: bfloat16 [16384, 512], P('ctx'), may hold values from -6 to 6
- attn_gate: bfloat16 [16384, 4096], P('ctx', 'mp'), may hold values from -6 to 6
- positions: int32 [16384], P('ctx'), may hold values from 0 to 4095, as said below
- block_lists: int32 [128, 13], P('ctx'), may hold values from -1 to 127, as said below
- out_weight: bfloat16 [2, 4096, 2048], P(None, 'mp', 'ctx'), may hold values from -0.09375 to 0.09375
Outputs:
- mixed: bfloat16 [16384, 2048], P('ctx', 'mp')
Inputs may be any that keep to these rules, and one draw needn't show every extreme that they name: `positions`: each entry is the token's offset from the first token of its document; documents follow one another. `block_lists`: row r starts with r itself, then distinct earlier blocks of the same shard of 256 tokens or of the 6 shards before it, then -1 for the unused entries; the number of used entries is ragged and some rows use all 13.
All inputs are finite; a program needn't handle non-finite values.
Results may differ from a plain program's by a relative error of at most 0.013.
Values may be sent and summed in bfloat16 or wider, within the bound.
A program may use at most 128 MiB of HBM per device.

v0:
```python
import jax
import jax.numpy as jnp
from jax import lax
from jax.sharding import PartitionSpec as P

DK = 128
AH = 16
KVH = 2
HA = 256
BLK = 128
STRETCH = 64
SPAN = 6
ROT = 64


def entering(value, axis, join, neutral):
    count, mine = (lax.axis_size(axis), lax.axis_index(axis))
    pieces = jax.tree.map(lambda part: lax.all_gather(part, axis), value)
    running = jax.tree.map(
        lambda part, zero: jnp.full_like(part, 0) + jnp.asarray(zero, part.dtype), value, neutral
    )

    def turn(position, running):
        longer = join(running, jax.tree.map(lambda part: part[position], pieces))
        return jax.tree.map(lambda new, old: jnp.where(position < mine, new, old), longer, running)

    return lax.fori_loop(0, count - 1, turn, running)


def shifted(block, axis, distance):
    devices = range(lax.axis_size(axis))
    route = [(i - distance, i) for i in devices if i - distance in devices]
    return lax.ppermute(block, axis, route)


def unit_rows(matrix):
    return matrix * lax.rsqrt(jnp.sum(matrix * matrix, -1, keepdims=True) + 1e-06)


def rotate_rows(matrix, locations):
    half = ROT // 2
    freq = jnp.power(jnp.float32(10000000.0), -2.0 * jnp.arange(half, dtype=jnp.float32) / ROT)
    angle = locations.astype(jnp.float32)[..., None] * freq
    cosine = jnp.cos(angle)
    sine = jnp.sin(angle)
    first = matrix[..., :half]
    second = matrix[..., half:ROT]
    return jnp.concatenate(
        [first * cosine - second * sine, second * cosine + first * sine, matrix[..., ROT:]], -1
    )


def lower_solve(matrix, target_rows):
    return lax.linalg.triangular_solve(
        matrix, target_rows, left_side=True, lower=True, unit_diagonal=True
    )


def delta_blocks(queries, keys_unit, values, write_rows, decay_rows, start, with_read):
    exact_result = lax.Precision.HIGHEST
    head_count, tok_rows, key_width = keys_unit.shape
    block_count = tok_rows // STRETCH

    def split_rows(matrix):
        if matrix.ndim == 2:
            return matrix.reshape(head_count, block_count, STRETCH).transpose(1, 0, 2)
        return matrix.reshape(head_count, block_count, STRETCH, matrix.shape[2]).transpose(
            1, 0, 2, 3
        )

    order = jnp.arange(STRETCH)
    strict_mask = order[:, None] > order[None, :]
    upto_mask = order[:, None] >= order[None, :]
    identity_c = jnp.eye(STRETCH, dtype=jnp.float32)

    def advance(recurrent_state, inputs):
        query_part, key_part, value_part, write_part, decay_part = inputs
        cumulative = jnp.cumsum(decay_part, axis=1)
        spread_log = cumulative[:, :, None] - cumulative[:, None, :]
        fade_strict = jnp.where(strict_mask, jnp.exp(jnp.where(strict_mask, spread_log, 0.0)), 0.0)
        key_gram = jnp.einsum("hck,hsk->hcs", key_part, key_part, precision=exact_result)
        lower_gram = write_part[:, :, None] * fade_strict * key_gram
        onset_fade = jnp.exp(cumulative)
        seen = jnp.einsum("hck,hkm->hcm", key_part, recurrent_state, precision=exact_result)
        target_rows = write_part[:, :, None] * (value_part - onset_fade[:, :, None] * seen)
        solved = lower_solve(lower_gram + identity_c, target_rows)
        finish_fade = jnp.exp(cumulative[:, -1:] - cumulative)
        new_state = jnp.exp(cumulative[:, -1])[:, None, None] * recurrent_state + jnp.einsum(
            "hsk,hsm->hkm", finish_fade[:, :, None] * key_part, solved, precision=exact_result
        )
        if with_read:
            fade_upto = jnp.where(upto_mask, jnp.exp(jnp.where(upto_mask, spread_log, 0.0)), 0.0)
            query_gram = (
                jnp.einsum("hck,hsk->hcs", query_part, key_part, precision=exact_result) * fade_upto
            )
            mixer_output = onset_fade[:, :, None] * jnp.einsum(
                "hck,hkm->hcm", query_part, recurrent_state, precision=exact_result
            )
            mixer_output = mixer_output + jnp.einsum(
                "hcs,hsm->hcm", query_gram, solved, precision=exact_result
            )
            return (new_state, mixer_output)
        return (new_state, None)

    inputs = (
        split_rows(queries),
        split_rows(keys_unit),
        split_rows(values),
        split_rows(write_rows),
        split_rows(decay_rows),
    )
    final, reads = lax.scan(advance, start, inputs)
    if with_read:
        reads = reads.transpose(1, 0, 2, 3).reshape(head_count, tok_rows, start.shape[2])
    return (final, reads)


def per_device(
    residual,
    delta_query,
    delta_key,
    delta_value,
    write_strength,
    log_decay,
    output_gate,
    norm_gain,
    attn_query,
    attn_key,
    attn_value,
    attn_gate,
    positions,
    block_lists,
    out_weight,
):
    exact_result = lax.Precision.HIGHEST
    tok_rows = residual.shape[0]
    head_count = log_decay.shape[0]
    val_width = norm_gain.shape[0]
    key_heads = delta_key.shape[1] // DK
    share = head_count // key_heads

    def head_major(matrix, count, width):
        return matrix.astype(jnp.float32).reshape(tok_rows, count, width).transpose(1, 0, 2)

    unit_query = jnp.repeat(unit_rows(head_major(delta_query, key_heads, DK)), share, axis=0)
    unit_key = jnp.repeat(unit_rows(head_major(delta_key, key_heads, DK)), share, axis=0)
    value_heads = head_major(delta_value, head_count, val_width)
    identity_k = jnp.broadcast_to(jnp.eye(DK, dtype=jnp.float32), (head_count, DK, DK))
    empty_push = jnp.zeros((head_count, DK, val_width), jnp.float32)
    start_both = jnp.concatenate([empty_push, identity_k], 2)
    values_both = jnp.concatenate(
        [value_heads, jnp.zeros((head_count, tok_rows, DK), jnp.float32)], 2
    )
    final_both, reads_both = delta_blocks(
        unit_query, unit_key, values_both, write_strength, log_decay, start_both, False
    )
    local_push = final_both[:, :, :val_width]
    local_lift = final_both[:, :, val_width:]

    def compose(earlier, later):
        lift_total = jnp.einsum("hij,hjk->hik", later[0], earlier[0], precision=exact_result)
        push_total = (
            jnp.einsum("hij,hjk->hik", later[0], earlier[1], precision=exact_result) + later[1]
        )
        return (lift_total, push_total)

    _, carried = entering((local_lift, local_push), "ctx", compose, (identity_k, empty_push))
    _, delta_read = delta_blocks(
        unit_query, unit_key, value_heads, write_strength, log_decay, carried, True
    )
    delta_read = delta_read.transpose(1, 0, 2)
    square_mean = jnp.mean(delta_read * delta_read, -1, keepdims=True)
    gate_rows = jax.nn.silu(
        output_gate.astype(jnp.float32).reshape(tok_rows, head_count, val_width)
    )
    delta_mixed = (
        (delta_read * lax.rsqrt(square_mean + 1e-06) * norm_gain * gate_rows)
        .astype(jnp.bfloat16)
        .reshape(tok_rows, head_count * val_width)
    )
    attn_heads = attn_gate.shape[1] // HA
    first_head = lax.axis_index("mp") * attn_heads
    pair_here = first_head // (AH // KVH)
    key_cols = lax.dynamic_slice_in_dim(attn_key, pair_here * HA, HA, 1)
    value_cols = lax.dynamic_slice_in_dim(attn_value, pair_here * HA, HA, 1)
    rotated_query = rotate_rows(
        attn_query.astype(jnp.float32).reshape(tok_rows, attn_heads, HA), positions[:, None]
    ).astype(jnp.bfloat16)
    rotated_key = rotate_rows(key_cols.astype(jnp.float32), positions).astype(jnp.bfloat16)
    packed = (rotated_key, value_cols)
    earlier_packs = []
    moving = packed
    for distance in range(SPAN):
        moving = shifted((moving[0], moving[1]), "ctx", 1)
        earlier_packs.append(moving)
    ordered = list(reversed(earlier_packs)) + [packed]
    keys_all = jnp.concatenate([member[0] for member in ordered], 0)
    values_all = jnp.concatenate([member[1] for member in ordered], 0)
    device_here = lax.axis_index("ctx")
    shard_blocks = tok_rows // BLK
    cand_count = (SPAN + 1) * shard_blocks
    candidates = (device_here - SPAN) * shard_blocks + jnp.arange(cand_count, dtype=jnp.int32)
    listed = jnp.any(block_lists[:, :, None] == candidates[None, None, :], axis=1) & (
        candidates[None, :] >= 0
    )
    listed_rows = jnp.repeat(jnp.repeat(listed, BLK, axis=0), BLK, axis=1)
    query_place = device_here * tok_rows + jnp.arange(tok_rows, dtype=jnp.int32)
    key_place = (device_here - SPAN) * tok_rows + jnp.arange(cand_count * BLK, dtype=jnp.int32)
    allowed = listed_rows & (key_place[None, :] <= query_place[:, None])
    scale = 1.0 / HA**0.5
    score = (
        jnp.einsum("qhd,kd->hqk", rotated_query, keys_all, preferred_element_type=jnp.float32)
        * scale
    )
    top = jnp.max(jnp.where(allowed[None], score, -jnp.inf), -1, keepdims=True)
    weights = jnp.where(allowed[None], jnp.exp(score - top), 0.0)
    weights_bf16 = weights.astype(jnp.bfloat16)
    numer = jnp.einsum("hqk,kd->qhd", weights_bf16, values_all, preferred_element_type=jnp.float32)
    denom = jnp.sum(weights, -1)
    attn_read = numer / denom.T[:, :, None]
    attn_mixed = (
        (
            attn_read
            * jax.nn.sigmoid(attn_gate.astype(jnp.float32).reshape(tok_rows, attn_heads, HA))
        )
        .astype(jnp.bfloat16)
        .reshape(tok_rows, attn_heads * HA)
    )
    piece = lax.all_gather(out_weight, "ctx", axis=2, tiled=True)
    terms = jnp.dot(delta_mixed, piece[0], preferred_element_type=jnp.float32) + jnp.dot(
        attn_mixed, piece[1], preferred_element_type=jnp.float32
    )
    summed = lax.psum_scatter(
        terms.astype(jnp.bfloat16), "mp", scatter_dimension=1, tiled=True
    ).astype(jnp.float32)
    return (residual.astype(jnp.float32) + summed).astype(jnp.bfloat16)


def solution(mesh):
    return jax.shard_map(
        per_device,
        mesh=mesh,
        in_specs=(
            P("ctx", "mp"),
            P("ctx", "mp"),
            P("ctx", "mp"),
            P("ctx", "mp"),
            P("mp", "ctx"),
            P("mp", "ctx"),
            P("ctx", "mp"),
            P(),
            P("ctx", "mp"),
            P("ctx", None),
            P("ctx", None),
            P("ctx", "mp"),
            P("ctx"),
            P("ctx", None),
            P(None, "mp", "ctx"),
        ),
        out_specs=P("ctx", "mp"),
        check_vma=False,
    )
```

profile of v0, /device:TPU:1, one launch (start us, length us, event | category | flops | bytes accessed | tf_op | source)
XLA Modules:
  0.0 742.5 jit_solution(13696352808664634739)
XLA Ops:
  13.0 92.1 %while.40 = (s32[]{:T(128)}, f32[4,128,256]{2,1,0:T(8,128)S(1)}, f32[4,4,64]{2,1,0:T(4,128)}, f32[4,4,64,128]{3,2,1,0:T(8,128)S(1)}, f32[4,4,64]{2,1,0:T(4,128)}...) while((s32[]{:T(128)}, f32[4,128,256]{2,1,0:T(8,128)S(1)}, ...), condition=%wide.region_3.4_spmd.clone.clone, body=%wide.region_1.3_spmd.clone.clone.sunk | while | flops 277487680 | bytes 3554493 | solution.py:112
  15.1 19.7 %custom-call.18 = f32[4,1,64,64]{2,3,1,0:T(8,128)S(1)} custom-call(f32[4,1,64,64]{3,2,1,0:T(8,128)S(1)} %fusion.172), custom_call_target="InvertDiagBlocksLowerTriangular" | custom-call | tf_op jit(solution)/shard_map/while/body/eval_jaxpr/triangular_solve | solution.py:54
  38.2 19.7 %custom-call.18 = f32[4,1,64,64]{2,3,1,0:T(8,128)S(1)} custom-call(f32[4,1,64,64]{3,2,1,0:T(8,128)S(1)} %fusion.172), custom_call_target="InvertDiagBlocksLowerTriangular" | custom-call | tf_op jit(solution)/shard_map/while/body/eval_jaxpr/triangular_solve | solution.py:54
  61.2 19.7 %custom-call.18 = f32[4,1,64,64]{2,3,1,0:T(8,128)S(1)} custom-call(f32[4,1,64,64]{3,2,1,0:T(8,128)S(1)} %fusion.172), custom_call_target="InvertDiagBlocksLowerTriangular" | custom-call | tf_op jit(solution)/shard_map/while/body/eval_jaxpr/triangular_solve | solution.py:54
  84.2 19.7 %custom-call.18 = f32[4,1,64,64]{2,3,1,0:T(8,128)S(1)} custom-call(f32[4,1,64,64]{3,2,1,0:T(8,128)S(1)} %fusion.172), custom_call_target="InvertDiagBlocksLowerTriangular" | custom-call | tf_op jit(solution)/shard_map/while/body/eval_jaxpr/triangular_solve | solution.py:54
  108.0 5.0 collective-permute-start.6
  114.0 3.6 collective-permute-start
  118.6 2.9 collective-permute-start.7
  122.3 5.4 collective-permute-start.1
  127.7 3.6 collective-permute-start.8
  131.4 4.0 collective-permute-start.2
  135.5 4.1 collective-permute-start.9
  145.4 3.5 collective-permute-start.3
  148.8 4.2 collective-permute-start.10
  153.0 4.1 collective-permute-start.4
  157.2 4.1 collective-permute-start.11
  161.3 1.7 fusion.103
  163.1 3.9 collective-permute-start.5
  175.1 1.9 fusion.119
  178.4 128.1 %all-gather.8.cloned.1.call-done = f32[256,128,128]{2,1,0:T(8,128)} async-done(((f32[4,128,128]{2,1,0:T(8,128)}), f32[256,128,128]{2,1,0:T(8,128)}) %all-gather.8.cloned.1.call-update) | async-done | bytes 16777232 | tf_op jit(solution)/shard_map/all_gather | solution.py:18
  306.5 192.9 %all-gather.10.cloned.1.call-done = f32[256,128,128]{2,1,0:T(8,128)} async-done(((f32[4,128,128]{2,1,0:T(8,128)}), f32[256,128,128]{2,1,0:T(8,128)}) %all-gather.10.cloned.1.call-update) | async-done | bytes 16777232 | tf_op jit(solution)/shard_map/all_gather | solution.py:18
  499.3 93.4 %while.42 = (s32[]{:T(128)}, f32[4,128,128]{2,1,0:T(8,128)S(1)}, s32[]{:T(128)}, f32[64,4,128,128]{3,2,1,0:T(8,128)}, f32[64,4,128,128]{3,2,1,0:T(8,128)}, /*index=5*/s32[]{:T(128)}, s32[]{:T(128)}) while((s32[]{:T(128)}, f32[4,128,128]{2,1,0:T(8,128)S(1)}, s32[]{:T(128)}, f32[64,4,128,128]{3,2,1,0:T(8,128)}, ...), condition=%wide.region_5.6_spmd.clone, body=%wide.region_4.5_spmd.clone.sunk | while | flops 100925440 | bytes 1837671 | solution.py:27
  499.4 1.5 fusion.194
  592.8 100.8 %while.41 = (s32[]{:T(128)}, f32[4,128,128]{2,1,0:T(8,128)S(1)}, f32[4,4,64,128]{3,2,0,1:T(8,128)S(1)}, f32[4,4,64]{2,1,0:T(4,128)}, f32[4,4,64,128]{3,2,1,0:T(8...) while((s32[]{:T(128)}, f32[4,128,128]{2,1,0:T(8,128)S(1)}, ...), condition=%wide.region_9.10_spmd.clone.clone, body=%wide.region_7.9_spmd.clone.clone.sunk | while | flops 252227648 | bytes 3443917 | solution.py:112
  595.9 20.4 %custom-call.19 = f32[4,1,64,64]{2,3,1,0:T(8,128)S(1)} custom-call(f32[4,1,64,64]{3,2,1,0:T(8,128)} %fusion.188), custom_call_target="InvertDiagBlocksLowerTriangular" | custom-call | tf_op jit(solution)/shard_map/while/body/eval_jaxpr/triangular_solve | solution.py:54
  621.1 20.4 %custom-call.19 = f32[4,1,64,64]{2,3,1,0:T(8,128)S(1)} custom-call(f32[4,1,64,64]{3,2,1,0:T(8,128)} %fusion.188), custom_call_target="InvertDiagBlocksLowerTriangular" | custom-call | tf_op jit(solution)/shard_map/while/body/eval_jaxpr/triangular_solve | solution.py:54
  646.3 20.4 %custom-call.19 = f32[4,1,64,64]{2,3,1,0:T(8,128)S(1)} custom-call(f32[4,1,64,64]{3,2,1,0:T(8,128)} %fusion.188), custom_call_target="InvertDiagBlocksLowerTriangular" | custom-call | tf_op jit(solution)/shard_map/while/body/eval_jaxpr/triangular_solve | solution.py:54
  671.5 20.4 %custom-call.19 = f32[4,1,64,64]{2,3,1,0:T(8,128)S(1)} custom-call(f32[4,1,64,64]{3,2,1,0:T(8,128)} %fusion.188), custom_call_target="InvertDiagBlocksLowerTriangular" | custom-call | tf_op jit(solution)/shard_map/while/body/eval_jaxpr/triangular_solve | solution.py:54
  695.0 2.5 fusion.78
  697.8 1.8 fusion.77
  699.6 34.8 %reduce-scatter.2.cloned.1.call-done = bf16[256,256]{1,0:T(8,128)(2,1)} async-done(((bf16[256,2048]{1,0:T(8,128)(2,1)}), bf16[256,256]{1,0:T(8,128)(2,1)}) %reduce-scatter.2.cloned.1.call-update) | async-done | bytes 131088 | tf_op jit(solution)/shard_map/reduce_scatter | solution.py:233
  734.4 1.6 add_convert_fusion
  (364 shorter events, 150.2 us)
Async XLA Ops:
  6.5 100.3 %copy-start = (bf16[256,512]{1,0:T(8,128)(2,1)S(1)}, bf16[256,512]{1,0:T(8,128)(2,1)}, u32[]{:S(2)}) copy-start(bf16[256,512]{1,0:T(8,128)(2,1)} %param.30) | copy-start | bytes 786436
  6.5 299.9 %all-gather.8.cloned.1.call-start = ((), (), s32[]{:S(2)}) async-start(), calls=%async_computation.3 | async-start | bytes 17039360 | tf_op jit(solution)/shard_map/all_gather | solution.py:18
  13.0 94.0 %copy-start.14 = (s32[256]{0:T(256)S(1)}, s32[256]{0:T(256)}, u32[]{:S(2)}) copy-start(s32[256]{0:T(256)} %param.33) | copy-start | bytes 3076
  105.1 12.6 %copy-start.10 = (bf16[256,512]{1,0:T(8,128)(2,1)S(1)}, bf16[256,512]{1,0:T(8,128)(2,1)}, u32[]{:S(2)}) copy-start(bf16[256,512]{1,0:T(8,128)(2,1)} %param.29) | copy-start | bytes 786436
  105.1 13.1 %copy-start.15 = (s32[2,13]{1,0:T(2,128)S(1)}, s32[2,13]{1,0:T(2,128)}, u32[]{:S(2)}) copy-start(s32[2,13]{1,0:T(2,128)} %param.34) | copy-start | bytes 316
  105.1 13.3 %copy-start.9 = (bf16[256,512]{1,0:T(8,128)(2,1)S(1)}, bf16[256,512]{1,0:T(8,128)(2,1)}, u32[]{:S(2)}) copy-start(bf16[256,512]{1,0:T(8,128)(2,1)} %param.32) | copy-start | bytes 786436
  106.0 393.3 %all-gather.10.cloned.1.call-start = ((), (), s32[]{:S(2)}) async-start(), calls=%async_computation.4 | async-start | bytes 17039360 | tf_op jit(solution)/shard_map/all_gather | solution.py:18
  106.8 588.1 %all-gather.6.cloned.1.call-start = ((), (), s32[]{:S(2)}) async-start(), calls=%async_computation.1 | async-start | bytes 4259840 | tf_op jit(solution)/shard_map/all_gather | solution.py:229
  108.0 10.6 %collective-permute-start.6 = (bf16[256,256]{0,1:T(8,128)(2,1)}, bf16[256,256]{0,1:T(8,128)(2,1)}, u32[]{:S(2)}, u32[]{:S(2)}) collective-permute-start(bf16[256,256]{0,1:T(8,128)(2,1)} %pad_maximum_fusion), channel_id=1, source_target_pairs={{0,8},{8,16},{16,24},{24,32},{32,40},{40,48},{48,56},{56,64},{64,7... | collective-permute-start | bytes 393224 | tf_op jit(solution)/shard_map/ppermute | solution.py:33
  114.0 28.1 %copy-start.5 = (bf16[256,256]{0,1:T(8,128)(2,1)}, bf16[256,256]{0,1:T(8,128)(2,1)S(1)}, u32[]{:S(2)}) copy-start(bf16[256,256]{0,1:T(8,128)(2,1)S(1)} %copy.165) | copy-start | bytes 393220
  114.0 8.3 %collective-permute-start = (bf16[256,256]{0,1:T(8,128)(2,1)S(1)}, bf16[256,256]{0,1:T(8,128)(2,1)}, u32[]{:S(2)}, u32[]{:S(2)}) collective-permute-start(bf16[256,256]{0,1:T(8,128)(2,1)S(1)} %copy.165), channel_id=1, source_target_pairs={{0,8},{8,16},{16,24},{24,32},{32,40},{40,48},{48,56},{56,64},{64,7... | collective-permute-start | bytes 393224 | tf_op jit(solution)/shard_map/ppermute | solution.py:33
  117.6 616.8 %reduce-scatter.2.cloned.1.call-start = ((), (), s32[]{:S(2)}) async-start(), calls=%async_computation.2 | async-start | bytes 1179648 | tf_op jit(solution)/shard_map/reduce_scatter | solution.py:233
  118.6 9.2 %collective-permute-start.7 = (bf16[256,256]{0,1:T(8,128)(2,1)}, bf16[256,256]{0,1:T(8,128)(2,1)S(1)}, u32[]{:S(2)}, u32[]{:S(2)}) collective-permute-start(bf16[256,256]{0,1:T(8,128)(2,1)} %collective-permute-done.6), channel_id=1, source_target_pairs={{0,8},{8,16},{16,24},{24,32},{32,40},{40,48},{48,56},{56,64},{64,7... | collective-permute-start | bytes 393224 | tf_op jit(solution)/shard_map/ppermute | solution.py:33
  122.3 9.1 %collective-permute-start.1 = (bf16[256,256]{0,1:T(8,128)(2,1)}, bf16[256,256]{0,1:T(8,128)(2,1)}, u32[]{:S(2)}, u32[]{:S(2)}) collective-permute-start(bf16[256,256]{0,1:T(8,128)(2,1)} %collective-permute-done), channel_id=1, source_target_pairs={{0,8},{8,16},{16,24},{24,32},{32,40},{40,48},{48,56},{56,64},{64,7... | collective-permute-start | bytes 393224 | tf_op jit(solution)/shard_map/ppermute | solution.py:33
  127.7 12.4 %copy-start.13 = (bf16[256,256]{0,1:T(8,128)(2,1)}, bf16[256,256]{0,1:T(8,128)(2,1)S(1)}, u32[]{:S(2)}) copy-start(bf16[256,256]{0,1:T(8,128)(2,1)S(1)} %collective-permute-done.7) | copy-start | bytes 393220
  127.7 7.7 %collective-permute-start.8 = (bf16[256,256]{0,1:T(8,128)(2,1)S(1)}, bf16[256,256]{0,1:T(8,128)(2,1)}, u32[]{:S(2)}, u32[]{:S(2)}) collective-permute-start(bf16[256,256]{0,1:T(8,128)(2,1)S(1)} %collective-permute-done.7), channel_id=1, source_target_pairs={{0,8},{8,16},{16,24},{24,32},{32,40},{40,48},{48,56},{56,64},{64,7... | collective-permute-start | bytes 393224 | tf_op jit(solution)/shard_map/ppermute | solution.py:33
  131.4 13.9 %collective-permute-start.2 = (bf16[256,256]{0,1:T(8,128)(2,1)}, bf16[256,256]{0,1:T(8,128)(2,1)}, u32[]{:S(2)}, u32[]{:S(2)}) collective-permute-start(bf16[256,256]{0,1:T(8,128)(2,1)} %collective-permute-done.1), channel_id=1, source_target_pairs={{0,8},{8,16},{16,24},{24,32},{32,40},{40,48},{48,56},{56,64},{64,7... | collective-permute-start | bytes 393224 | tf_op jit(solution)/shard_map/ppermute | solution.py:33
  135.5 13.4 %collective-permute-start.9 = (bf16[256,256]{0,1:T(8,128)(2,1)}, bf16[256,256]{0,1:T(8,128)(2,1)}, u32[]{:S(2)}, u32[]{:S(2)}) collective-permute-start(bf16[256,256]{0,1:T(8,128)(2,1)} %collective-permute-done.8), channel_id=1, source_target_pairs={{0,8},{8,16},{16,24},{24,32},{32,40},{40,48},{48,56},{56,64},{64,7... | collective-permute-start | bytes 393224 | tf_op jit(solution)/shard_map/ppermute | solution.py:33
  142.2 31.9 %copy-start.6 = (bf16[256,256]{0,1:T(8,128)(2,1)S(1)}, bf16[256,256]{0,1:T(8,128)(2,1)}, u32[]{:S(2)}) copy-start(bf16[256,256]{0,1:T(8,128)(2,1)} %copy-done.5) | copy-start | bytes 393220
  142.2 32.0 %copy-start.7 = (bf16[256,2,32]{2,0,1:T(8,128)(2,1)S(1)}, bf16[256,2,32]{2,0,1:T(8,128)(2,1)}, u32[]{:S(2)}) copy-start(bf16[256,2,32]{2,0,1:T(8,128)(2,1)} %get-tuple-element.436) | copy-start | bytes 98308
  143.2 31.0 %copy-start.3 = (bf16[256,2,192]{2,0,1:T(8,128)(2,1)S(1)}, bf16[256,2,192]{2,0,1:T(8,128)(2,1)}, u32[]{:S(2)}) copy-start(bf16[256,2,192]{2,0,1:T(8,128)(2,1)} %slice.68) | copy-start | bytes 589828
  143.2 31.0 %copy-start.8 = (bf16[256,2,32]{2,0,1:T(8,128)(2,1)S(1)}, bf16[256,2,32]{2,0,1:T(8,128)(2,1)}, u32[]{:S(2)}) copy-start(bf16[256,2,32]{2,0,1:T(8,128)(2,1)} %get-tuple-element.437) | copy-start | bytes 98308
  145.4 7.7 %collective-permute-start.3 = (bf16[256,256]{0,1:T(8,128)(2,1)}, bf16[256,256]{0,1:T(8,128)(2,1)S(1)}, u32[]{:S(2)}, u32[]{:S(2)}) collective-permute-start(bf16[256,256]{0,1:T(8,128)(2,1)} %collective-permute-done.2), channel_id=1, source_target_pairs={{0,8},{8,16},{16,24},{24,32},{32,40},{40,48},{48,56},{56,64},{64,7... | collective-permute-start | bytes 393224 | tf_op jit(solution)/shard_map/ppermute | solution.py:33
  148.8 8.4 %collective-permute-start.10 = (bf16[256,256]{0,1:T(8,128)(2,1)}, bf16[256,256]{0,1:T(8,128)(2,1)S(1)}, u32[]{:S(2)}, u32[]{:S(2)}) collective-permute-start(bf16[256,256]{0,1:T(8,128)(2,1)} %collective-permute-done.9), channel_id=1, source_target_pairs={{0,8},{8,16},{16,24},{24,32},{32,40},{40,48},{48,56},{56,64},{64,7... | collective-permute-start | bytes 393224 | tf_op jit(solution)/shard_map/ppermute | solution.py:33
  153.0 10.0 %collective-permute-start.4 = (bf16[256,256]{0,1:T(8,128)(2,1)S(1)}, bf16[256,256]{0,1:T(8,128)(2,1)S(1)}, u32[]{:S(2)}, u32[]{:S(2)}) collective-permute-start(bf16[256,256]{0,1:T(8,128)(2,1)S(1)} %collective-permute-done.3), channel_id=1, source_target_pairs={{0,8},{8,16},{16,24},{24,32},{32,40},{40,48},{48,56},{56,64},{64,7... | collective-permute-start | bytes 393224 | tf_op jit(solution)/shard_map/ppermute | solution.py:33
  157.2 9.7 %collective-permute-start.11 = (bf16[256,256]{0,1:T(8,128)(2,1)S(1)}, bf16[256,256]{0,1:T(8,128)(2,1)S(1)}, u32[]{:S(2)}, u32[]{:S(2)}) collective-permute-start(bf16[256,256]{0,1:T(8,128)(2,1)S(1)} %collective-permute-done.10), channel_id=1, source_target_pairs={{0,8},{8,16},{16,24},{24,32},{32,40},{40,48},{48,56},{56,64},{64,7... | collective-permute-start | bytes 393224 | tf_op jit(solution)/shard_map/ppermute | solution.py:33
  163.1 8.3 %collective-permute-start.5 = (bf16[256,256]{0,1:T(8,128)(2,1)S(1)}, bf16[256,256]{0,1:T(8,128)(2,1)S(1)}, u32[]{:S(2)}, u32[]{:S(2)}) collective-permute-start(bf16[256,256]{0,1:T(8,128)(2,1)S(1)} %collective-permute-done.4), channel_id=1, source_target_pairs={{0,8},{8,16},{16,24},{24,32},{32,40},{40,48},{48,56},{56,64},{64,7... | collective-permute-start | bytes 393224 | tf_op jit(solution)/shard_map/ppermute | solution.py:33
  175.1 1.9 copy-start.4
  499.3 93.4 %copy-start.2 = (f32[2,256,128]{2,1,0:T(8,128)S(1)}, f32[2,256,128]{2,1,0:T(8,128)}, u32[]{:S(2)}) copy-start(f32[2,256,128]{2,1,0:T(8,128)} %fusion.103) | copy-start | bytes 786436
  693.6 3.8 copy-start.11
  694.9 2.8 copy-start.1
  697.5 36.9 %copy-start.12 = (bf16[256,256]{1,0:T(8,128)(2,1)S(1)}, bf16[256,256]{1,0:T(8,128)(2,1)}, u32[]{:S(2)}) copy-start(bf16[256,256]{1,0:T(8,128)(2,1)} %param.21) | copy-start | bytes 393220
Sparse Core Ops, SparseCore 0:
  106.2 200.2 all-gather.7
  309.4 189.8 all-gather.9
  502.3 135.8 all-gather.5
  699.7 34.6 reduce-scatter.1
where the time goes:
time: 746 us; the launch traced here: 742 us
  waiting for transfers between devices  357 us (48%)
  other arithmetic  177 us (24%)
  matrix products  118 us (16%)
  starting transfers between devices  48.5 us (7%)
  local copies, waits for them, and re-layouts  25.1 us (3%)
  between operations  13.8 us (2%)
    all_gather x2, waiting for transfers between devices, entering(): pieces = jax.tree.map(lambda part: lax.all_gather(part, axis), value)  321 us
    another operation x24, other arithmetic, lower_solve(): lax.linalg.triangular_solve(matrix, target_rows, left_side=True, lower=Tr...  160 us
    dot_general x63, matrix products, compose(): jnp.einsum('hij,hjk->hik', later[0], earlier[1], precision=exact_result)  89.7 us
    ppermute x12, starting transfers between devices, shifted(): return lax.ppermute(block, axis, route)  48.3 us
    reduce_scatter x1, waiting for transfers between devices, per_device(): lax.psum_scatter(terms.astype(jnp.bfloat16), 'mp', scatter_dimension=1, t...  34.8 us
  transfers between devices with their start and end apart: 16, of which 5 were waited for; matrix products, arithmetic and copies ran while one was open for 29% of the time, Pallas kernels for 0%

commit v1 on v0

v1 whole, which is shorter than its diff:
```python
import functools

import jax
import jax.numpy as jnp
from jax import lax
from jax.experimental import pallas as pl
from jax.experimental.pallas import tpu as pltpu
from jax.sharding import PartitionSpec as P

DK = 128
AH = 16
KVH = 2
HA = 256
BLK = 128
SPAN = 6
ROT = 64
TOK = 256
ZN = 16
YN = 4
GRP = 4
MAPR = 144
LOGICAL = pl.DeviceIdType.MESH
F32 = jnp.float32
BF16 = jnp.bfloat16
VMEM = pl.BlockSpec(memory_space=pltpu.VMEM)
MB = 1 << 20


def dot(a, b):
    return jnp.dot(a, b, preferred_element_type=F32)


def dot_nt(a, b):
    return lax.dot_general(a, b, (((1,), (1,)), ((), ())), preferred_element_type=F32)


def split2(a):
    high = a.astype(BF16)
    return high, (a - high.astype(F32)).astype(BF16)


def dot3(a, b):
    ah, al = split2(a)
    bh, bl = split2(b)
    return dot(ah, bh) + (dot(ah, bl) + dot(al, bh))


def iota(shape, axis):
    return lax.broadcasted_iota(jnp.int32, shape, axis)


def block_inverse(lower):
    row = iota((TOK, 128), 0)
    lane = iota((TOK, 128), 1)
    left = jnp.where(row // 16 == lane // 16, lower[:, :128], 0.0)
    right = jnp.where(row // 16 == (lane + 128) // 16, lower[:, 128:], 0.0)
    folded = left + right
    for step in (64, 32, 16):
        folded = folded + pltpu.roll(folded, step, 1)
    low3 = folded.reshape(16, 16, 128)
    inv3 = jnp.where(row % 16 == lane % 16, 1.0, 0.0).astype(F32).reshape(16, 16, 128)
    for j in range(15):
        inv3 = inv3 - low3[:, :, j : j + 1] * inv3[:, j : j + 1, :]
    compact = inv3.reshape(TOK, 128)
    r1 = iota((128, 128), 0)
    c1 = iota((128, 128), 1)
    halves = []
    for part in range(2):
        rows = slice(part * 128, part * 128 + 128)
        inv = jnp.where(r1 // 16 == c1 // 16, compact[rows], 0.0)
        low = lower[rows, rows]
        for size in (16, 32, 64):
            between = (r1 // (2 * size) == c1 // (2 * size)) & (r1 // size != c1 // size)
            off = jnp.where(between, low, 0.0)
            inv = inv - dot3(inv, dot3(off, inv))
        halves.append(inv)
    cross = -dot3(halves[1], dot3(lower[128:, :128], halves[0]))
    top = jnp.concatenate([halves[0], jnp.zeros((128, 128), F32)], 1)
    return jnp.concatenate([top, jnp.concatenate([cross, halves[1]], 1)], 0)


def local_kernel(
    dq_ref, dk_ref, dv_ref, wr_ref, ld_ref, aq_ref, ak_ref, av_ref, turn_ref,
    maps_ref, r0_ref, qe_ref, qrot_ref, kv_ref,
):
    rr = iota((TOK, TOK), 0)
    cc = iota((TOK, TOK), 1)
    upto = rr >= cc
    strict = rr > cc
    diag = rr == cc
    decay = ld_ref[...]
    tri = jnp.where(rr <= cc, 1.0, 0.0).astype(F32)
    exact = lax.Precision.HIGHEST
    g_rows = jnp.dot(decay, tri, precision=exact, preferred_element_type=F32)
    g_cols = jnp.transpose(jnp.concatenate([g_rows, g_rows], 0))
    b_cols = jnp.transpose(jnp.concatenate([wr_ref[...], wr_ref[...]], 0))
    for kh in range(2):
        cols = slice(kh * DK, kh * DK + DK)
        kb = dk_ref[:, cols]
        qb = dq_ref[:, cols]
        qf = qb.astype(F32)
        gram = dot_nt(kb, kb)
        mixed = dot_nt(qb, kb)
        square = jnp.where(diag, gram, 0.0)
        rk_col = lax.rsqrt(jnp.sum(square, 1, keepdims=True) + 1e-06)
        rk_row = lax.rsqrt(jnp.sum(square, 0, keepdims=True) + 1e-06)
        rq_col = lax.rsqrt(jnp.sum(qf * qf, 1, keepdims=True) + 1e-06)
        kt = jnp.transpose(kb.astype(F32)).astype(BF16)
        for sub in range(2):
            h = kh * 2 + sub
            g_row = g_rows[h : h + 1]
            g_col = g_cols[:, h : h + 1]
            b_row = wr_ref[h : h + 1, :]
            b_col = b_cols[:, h : h + 1]
            fade = jnp.where(upto, jnp.exp(jnp.where(upto, g_col - g_row, 0.0)), 0.0)
            lower = jnp.where(strict, fade * gram, 0.0) * (b_col * rk_col) * rk_row
            inv = block_inverse(lower)
            vb = dv_ref[:, h * DK : h * DK + DK]
            th, tl = split2(inv * b_row)
            u = dot(th, vb) + dot(tl, vb)
            th, tl = split2(inv * (b_row * jnp.exp(g_row) * rk_row))
            w = dot(th, kb) + dot(tl, kb)
            both = jnp.concatenate([w, u], 1)
            g_end = g_col[TOK - 1 : TOK]
            pushed = (both * (jnp.exp(g_end - g_col) * rk_col)).astype(BF16)
            maps_ref[h, :DK, :] = dot(kt, pushed).astype(BF16)
            maps_ref[h, DK:, :] = gamma_rows(jnp.broadcast_to(jnp.exp(g_end), (1, 2 * DK)))
            reads = (fade * mixed * rq_col * rk_row).astype(BF16)
            seen = dot(reads, both.astype(BF16))
            r0_ref[h] = seen[:, DK:]
            qe_ref[h] = (jnp.exp(g_col) * rq_col * qf - seen[:, :DK]).astype(BF16)
    cosine = turn_ref[:, :128]
    sine = turn_ref[:, 128:]
    lane = iota((TOK, 128), 1)

    def rotate(x):
        swapped = jnp.where(lane < ROT // 2, pltpu.roll(x, 128 - ROT // 2, 1), pltpu.roll(x, ROT // 2, 1))
        return x * cosine + swapped * sine

    for head in range(2):
        rows = slice(head * TOK, head * TOK + TOK)
        first = aq_ref[:, head * HA : head * HA + 128].astype(F32)
        turned = rotate(first).astype(BF16)
        qrot_ref[rows, :128] = turned * BF16(1.0 / 16)
        qrot_ref[rows, 128:] = aq_ref[:, head * HA + 128 : head * HA + HA] * BF16(1.0 / 16)
    pair = lax.axis_index("mp") // 4
    keys = jnp.where(pair == 0, ak_ref[:, :HA], ak_ref[:, HA:])
    values = jnp.where(pair == 0, av_ref[:, :HA], av_ref[:, HA:])
    turned = rotate(keys[:, :128].astype(F32)).astype(BF16)
    for half in range(2):
        rows = slice(half * 128, half * 128 + 128)
        kv_ref[half, :128, :128] = turned[rows]
        kv_ref[half, :128, 128:] = keys[rows, 128:]
        kv_ref[half, 128:, :] = values[rows]


def gamma_rows(gamma):
    high = gamma.astype(BF16).astype(F32)
    middle = (gamma - high).astype(BF16).astype(F32)
    low = gamma - high - middle
    row = iota((16, gamma.shape[1]), 0)
    rows = jnp.where(row == 0, high, jnp.where(row == 1, middle, jnp.where(row == 2, low, 0.0)))
    return rows.astype(BF16)


def read_map(ref, index):
    tail = ref[index, DK:, :].astype(F32)
    gamma = tail[0:1] + tail[1:2] + tail[2:3]
    return gamma, ref[index, :DK, :].astype(F32)


def join(later, earlier):
    gl, xl = later
    ge, xe = earlier
    scaled = jnp.concatenate([xl[:, :DK] * ge[:, :DK], xl[:, DK:]], 1)
    return gl * ge, gl * xe + scaled - dot(xl[:, :DK].astype(BF16), xe.astype(BF16))


def apply_map(one, state):
    gamma, x = one
    return gamma[:, :DK] * state + x[:, DK:] - dot(x[:, :DK].astype(BF16), state.astype(BF16))


def write_map(ref, index, one):
    gamma, x = one
    ref[index, :DK, :] = x.astype(BF16)
    ref[index, DK:, :] = gamma_rows(gamma)


def chosen(index, options):
    result = options[0]
    for number in range(1, len(options)):
        result = jax.tree.map(lambda a, b: jnp.where(index == number, b, a), result, options[number])
    return result


def scan_kernel(
    maps_ref, qrot_ref, kv_ref, bias_ref, gate_ref,
    state_ref, attn_ref,
    l1, l2, l3, pre, pregam, ssend, sgot, kvbuf, m_scr, l_scr, acc,
    s1, r1, s2, r2, s3, r3, s4, r4, kzs, kzr, kcs, kcr,
):
    c = lax.axis_index("ctx")
    mp = lax.axis_index("mp")
    y = c // ZN
    z = c % ZN
    zlo = z % GRP
    zhi = z // GRP
    core = mp % 2
    sibling = mp + 1 - 2 * core
    after = (c + 1) % (ZN * YN)
    before = (c + ZN * YN - 1) % (ZN * YN)

    def lo_peer(d):
        return (zlo + d) % GRP

    def lo_dev(d):
        return (y * ZN + zhi * GRP + lo_peer(d), mp)

    def hi_dev(d):
        return (y * ZN + ((zhi + d) % GRP) * GRP + zlo, mp)

    def y_dev(d):
        return (((y + d) % YN) * ZN + z, mp)

    barrier = pltpu.get_barrier_semaphore()
    peers = [f(d) for f in (lo_dev, hi_dev, y_dev) for d in (1, 2, 3)]
    peers += [(after, mp), (before, mp), (c, sibling)]
    for peer in peers:
        pl.semaphore_signal(barrier, inc=1, device_id=peer, device_id_type=LOGICAL)
    pl.semaphore_wait(barrier, len(peers))

    def remote(src, dst, send, recv, device):
        return pltpu.make_async_remote_copy(
            src_ref=src, dst_ref=dst, send_sem=send, recv_sem=recv, device_id=device, device_id_type=LOGICAL
        )

    def c1(d):
        return remote(maps_ref.at[lo_peer(d)], l1.at[zlo], s1.at[d - 1], r1.at[d - 1], lo_dev(d))

    def c2(d):
        return remote(l2.at[zhi], l2.at[zhi], s2.at[d - 1], r2.at[d - 1], hi_dev(d))

    def c3(d):
        return remote(l3.at[y], l3.at[y], s3.at[d - 1], r3.at[d - 1], y_dev(d))

    def c4(d):
        return remote(ssend.at[lo_peer(d)], sgot.at[zlo], s4.at[d - 1], r4.at[d - 1], lo_dev(d))

    def kz(s):
        src = kv_ref.at[core] if s == 1 else kvbuf.at[s - 2, core]
        return remote(src, kvbuf.at[s - 1, core], kzs.at[s - 1], kzr.at[s - 1], (after, mp))

    def kc(s):
        return remote(kvbuf.at[s - 1, core], kvbuf.at[s - 1, core], kcs.at[s - 1], kcr.at[s - 1], (c, sibling))

    def kv_step(s):
        kz(s).wait_recv()
        if s < SPAN:
            kz(s + 1).start()
        kc(s).start()

    def attend(s):
        first = s == 0
        qk = []
        for half in range(2):
            keys = kv_ref[half, :128, :] if first else kvbuf[s - 1, half, :128, :]
            qk.append(dot_nt(qrot_ref[...], keys))
        score = jnp.concatenate(qk, 1)
        rows = bias_ref[2 * s : 2 * s + 2, :]
        bias = jnp.concatenate(
            [jnp.broadcast_to(rows[qb : qb + 1], (BLK, TOK)) for _ in range(2) for qb in range(2)], 0
        )
        score = score + bias
        if first:
            r = iota((2 * TOK, TOK), 0) % TOK
            score = jnp.where(iota((2 * TOK, TOK), 1) <= r, score, -1e30)
        top = jnp.max(score, 1, keepdims=True)
        if not first:
            old = m_scr[...]
            top = jnp.maximum(old, top)
            fade = jnp.exp(old - top)
        weights = jnp.exp(score - top)
        total = jnp.sum(weights, 1, keepdims=True)
        wb = weights.astype(BF16)
        part = None
        for half in range(2):
            values = kv_ref[half, 128:, :] if first else kvbuf[s - 1, half, 128:, :]
            term = dot(wb[:, half * 128 : half * 128 + 128], values)
            part = term if part is None else part + term
        m_scr[...] = top
        if first:
            l_scr[...] = total
            acc[...] = part
        else:
            l_scr[...] = l_scr[...] * fade + total
            acc[...] = acc[...] * fade + part

    for d in (2, 1, 3):
        c1(d).start()
    kz(1).start()
    l1[zlo] = maps_ref[zlo]
    attend(0)
    for d in (1, 2, 3):
        c1(d).wait_recv()
    run = read_map(l1, 0)
    for i in range(1, GRP):
        pre[i - 1] = run[1]
        pregam[i - 1] = run[0]
        run = join(read_map(l1, i), run)
    write_map(l2, zhi, run)
    for d in (2, 1, 3):
        c2(d).start()
    kv_step(1)
    kv_step(2)
    kc(1).wait_recv()
    attend(1)
    kv_step(3)
    kc(2).wait_recv()
    attend(2)
    for d in (1, 2, 3):
        c2(d).wait_recv()
    ones = jnp.ones((1, 2 * DK), F32)
    rps = [(ones, jnp.zeros((DK, 2 * DK), F32)), read_map(l2, 0)]
    for i in range(1, GRP):
        rps.append(join(read_map(l2, i), rps[-1]))
    write_map(l3, y, rps[GRP])
    for d in (2, 1, 3):
        c3(d).start()
    mine = chosen(zhi, rps[:GRP])
    kv_step(4)
    kc(3).wait_recv()
    attend(3)
    for d in (1, 2, 3):
        c3(d).wait_recv()
    carries = [jnp.zeros((DK, DK), F32), read_map(l3, 0)[1][:, DK:]]
    for i in range(1, YN - 1):
        carries.append(apply_map(read_map(l3, i), carries[-1]))
    carry = apply_map(mine, chosen(y, carries))
    ssend[0] = carry.astype(BF16)
    for i in range(1, GRP):
        ssend[i] = apply_map((pregam[i - 1], pre[i - 1]), carry).astype(BF16)
    for d in (2, 1, 3):
        c4(d).start()
    sgot[zlo] = ssend[zlo]
    kv_step(5)
    kc(4).wait_recv()
    attend(4)
    kv_step(6)
    kc(5).wait_recv()
    attend(5)
    kc(6).wait_recv()
    attend(6)
    for head in range(2):
        rows = slice(head * TOK, head * TOK + TOK)
        cols = slice(head * HA, head * HA + HA)
        gate = gate_ref[:, cols].astype(F32)
        read = acc[rows, :] / l_scr[rows, :]
        attn_ref[:, cols] = (read / (1.0 + jnp.exp(-gate))).astype(BF16)
    for d in (1, 2, 3):
        c4(d).wait_recv()
    state_ref[...] = sgot[...]
    for d in (1, 2, 3):
        c1(d).wait_send()
        c2(d).wait_send()
        c3(d).wait_send()
        c4(d).wait_send()
    for s in range(1, SPAN + 1):
        kz(s).wait_send()
        kc(s).wait_send()


def final_kernel(
    state_ref, r0_ref, qe_ref, gate_ref, gain_ref, attn_ref, weight_ref,
    out_ref,
    mixed, sbuf, rbuf, ss, rs,
):
    c = lax.axis_index("ctx")
    mp = lax.axis_index("mp")

    def dev(d):
        return (c, (mp + d) % 8)

    barrier = pltpu.get_barrier_semaphore()
    for d in range(1, 8):
        pl.semaphore_signal(barrier, inc=1, device_id=dev(d), device_id_type=LOGICAL)
    for h in range(4):
        cols = slice(h * DK, h * DK + DK)
        read = r0_ref[h] + dot(qe_ref[h], state_ref[h])
        scale = lax.rsqrt(jnp.mean(read * read, 1, keepdims=True) + 1e-06)
        gate = gate_ref[:, cols].astype(F32)
        silu = gate / (1.0 + jnp.exp(-gate))
        mixed[:, cols] = (read * scale * gain_ref[...] * silu).astype(BF16)
    pl.semaphore_wait(barrier, 7)

    def copy(d):
        return pltpu.make_async_remote_copy(
            src_ref=sbuf.at[d - 1],
            dst_ref=rbuf.at[d - 1],
            send_sem=ss.at[d - 1],
            recv_sem=rs.at[d - 1],
            device_id=dev(d),
            device_id_type=LOGICAL,
        )

    def term(d):
        to = (mp + d) % 8
        first = weight_ref[to, :, 0].reshape(256, 512)
        second = weight_ref[to, :, 1].reshape(256, 512)
        return (dot_nt(mixed[...], first) + dot_nt(attn_ref[...], second)).astype(BF16)

    for d in (4, 3, 5, 2, 6, 1, 7):
        sbuf[d - 1] = term(d)
        copy(d).start()
    total = term(0).astype(F32)
    for d in (4, 3, 5, 2, 6, 1, 7):
        copy(d).wait_recv()
        total = total + rbuf[d - 1].astype(F32)
    out_ref[...] = total
    for d in range(1, 8):
        copy(d).wait_send()


def per_device(
    residual,
    delta_query,
    delta_key,
    delta_value,
    write_strength,
    log_decay,
    output_gate,
    norm_gain,
    attn_query,
    attn_key,
    attn_value,
    attn_gate,
    positions,
    block_lists,
    out_weight,
):
    weight_rows = jnp.transpose(out_weight, (2, 0, 1))
    weight_all = lax.all_gather(weight_rows, "ctx", axis=0, tiled=True)
    weight_all = weight_all.reshape(8, 8, 32, 2, 512).transpose(0, 1, 3, 2, 4)

    half = ROT // 2
    freq = jnp.power(jnp.float32(10000000.0), -2.0 * jnp.arange(half, dtype=F32) / ROT)
    angle = positions.astype(F32)[:, None] * freq
    cosine = jnp.cos(angle)
    sine = jnp.sin(angle)
    ones = jnp.ones((TOK, 128 - ROT), F32)
    turn = jnp.concatenate([cosine, cosine, ones, -sine, sine, 0 * ones], 1)

    here = lax.axis_index("ctx")
    candidates = (here[None] - jnp.arange(SPAN + 1, dtype=jnp.int32))[:, None] * 2 + jnp.arange(2, dtype=jnp.int32)
    listed = jnp.any(block_lists[None, :, None, :] == candidates[:, None, :, None], -1)
    listed = listed & (candidates >= 0)[:, None, :]
    bias = jnp.where(listed, 0.0, -1e30).astype(F32)
    bias = jnp.repeat(bias, BLK, axis=2).reshape(2 * (SPAN + 1), TOK)
    bias = jnp.concatenate([bias, jnp.zeros((2, TOK), F32)], 0)

    shape = jax.ShapeDtypeStruct
    maps, r0, qe, qrot, kv = pl.pallas_call(
        local_kernel,
        out_shape=(
            shape((4, MAPR, 2 * DK), BF16),
            shape((4, TOK, DK), F32),
            shape((4, TOK, DK), BF16),
            shape((2 * TOK, HA), BF16),
            shape((2, TOK, HA), BF16),
        ),
        in_specs=[VMEM] * 9,
        out_specs=(VMEM,) * 5,
        compiler_params=pltpu.CompilerParams(vmem_limit_bytes=48 * MB),
        cost_estimate=pl.CostEstimate(flops=2 * 10**9, bytes_accessed=4 * 10**6, transcendentals=10**6),
        name="delta_local",
    )(delta_query, delta_key, delta_value, write_strength, log_decay, attn_query, attn_key, attn_value, turn)

    dma = pltpu.SemaphoreType.DMA
    state, attn_mixed = pl.pallas_call(
        scan_kernel,
        out_shape=(shape((4, DK, DK), BF16), shape((TOK, 2 * HA), BF16)),
        in_specs=[VMEM] * 5,
        out_specs=(VMEM,) * 2,
        scratch_shapes=[
            pltpu.VMEM((GRP, MAPR, 2 * DK), BF16),
            pltpu.VMEM((GRP, MAPR, 2 * DK), BF16),
            pltpu.VMEM((YN, MAPR, 2 * DK), BF16),
            pltpu.VMEM((GRP - 1, DK, 2 * DK), F32),
            pltpu.VMEM((GRP - 1, 1, 2 * DK), F32),
            pltpu.VMEM((GRP, DK, DK), BF16),
            pltpu.VMEM((GRP, DK, DK), BF16),
            pltpu.VMEM((SPAN, 2, TOK, HA), BF16),
            pltpu.VMEM((2 * TOK, 1), F32),
            pltpu.VMEM((2 * TOK, 1), F32),
            pltpu.VMEM((2 * TOK, HA), F32),
        ]
        + [dma((3,))] * 8
        + [dma((SPAN,))] * 4,
        compiler_params=pltpu.CompilerParams(
            vmem_limit_bytes=48 * MB, collective_id=1, has_side_effects=True
        ),
        cost_estimate=pl.CostEstimate(flops=2 * 10**9, bytes_accessed=10**8, transcendentals=10**6),
        name="scan_attend",
    )(maps, qrot, kv, bias, attn_gate)

    summed = pl.pallas_call(
        final_kernel,
        out_shape=shape((TOK, 256), F32),
        in_specs=[VMEM] * 7,
        out_specs=VMEM,
        scratch_shapes=[
            pltpu.VMEM((TOK, 4 * DK), BF16),
            pltpu.VMEM((7, TOK, 256), BF16),
            pltpu.VMEM((7, TOK, 256), BF16),
            dma((7,)),
            dma((7,)),
        ],
        compiler_params=pltpu.CompilerParams(
            vmem_limit_bytes=48 * MB, collective_id=2, has_side_effects=True
        ),
        name="project_sum",
    )(state, r0, qe, output_gate, norm_gain.reshape(1, DK), attn_mixed, weight_all)
    return (residual.astype(F32) + summed).astype(BF16)


def solution(mesh):
    return jax.shard_map(
        per_device,
        mesh=mesh,
        in_specs=(
            P("ctx", "mp"),
            P("ctx", "mp"),
            P("ctx", "mp"),
            P("ctx", "mp"),
            P("mp", "ctx"),
            P("mp", "ctx"),
            P("ctx", "mp"),
            P(),
            P("ctx", "mp"),
            P("ctx", None),
            P("ctx", None),
            P("ctx", "mp"),
            P("ctx"),
            P("ctx", None),
            P(None, "mp", "ctx"),
        ),
        out_specs=P("ctx", "mp"),
        check_vma=False,
    )
```

time: 746 us -> 197 us (0.26)
  waiting for transfers between devices: 357 us -> 67 us
  other arithmetic: 177 us -> 2.83 us
  matrix products: 118 us -> 0 us
  Pallas kernels: 0 us -> 103 us
  starting transfers between devices: 48.5 us -> 0.01 us
  local copies, waits for them, and re-layouts: 25.1 us -> 10.3 us
    all_gather x3 -> x1, waiting for transfers between devices: 321 us -> 66.3 us  [per_device(): weight_all = lax.all_gather(weight_rows, 'ctx', axis=0, tiled=True)]
    another operation x33 -> x0, other arithmetic: 163 us -> none  [the longest x24 160 us: lower_solve(): lax.linalg.triangular_solve(matrix, target_rows, left_side=True, lower=Tr...]
    dot_general x103 -> x0, matrix products: 115 us -> none  [the longest x63 89.7 us: compose(): jnp.einsum('hij,hjk->hik', later[0], earlier[1], precision=exact_result)]
    pallas_call x0 -> x3, Pallas kernels: none -> 103 us  [the longest x1 65.7 us: per_device(): pl.pallas_call(scan_kernel, out_shape=(shape((4, DK, DK), BF16), shape((T...]
    ppermute x12 -> x0, starting transfers between devices: 48.3 us -> none  [shifted(): return lax.ppermute(block, axis, route)]
    reduce_scatter x1 -> x0, waiting for transfers between devices: 34.8 us -> none  [per_device(): lax.psum_scatter(terms.astype(jnp.bfloat16), 'mp', scatter_dimension=1, t...]
  transfers between devices with their start and end apart: 16 -> 1, of which waited for: 5 -> 1; matrix products, arithmetic and copies ran while one was open for 29% -> 1% of each run, Pallas kernels for 0% -> 39%
where the time goes in v1:
time: 197 us; the launch traced here: 196 us
  Pallas kernels  103 us (52%)
  waiting for transfers between devices  67 us (34%)
  between operations  13.6 us (7%)
  local copies, waits for them, and re-layouts  10.3 us (5%)
  other arithmetic  2.83 us (1%)
    all_gather x1, waiting for transfers between devices, per_device(): weight_all = lax.all_gather(weight_rows, 'ctx', axis=0, tiled=True)  66.3 us
    pallas_call x1, Pallas kernels, per_device(): pl.pallas_call(scan_kernel, out_shape=(shape((4, DK, DK), BF16), shape((T...  65.7 us
    pallas_call x1, Pallas kernels, per_device(): pl.pallas_call(final_kernel, out_shape=shape((TOK, 256), F32), in_specs=[...  25.7 us
    pallas_call x1, Pallas kernels, per_device(): pl.pallas_call(local_kernel, out_shape=(shape((4, MAPR, 2 * DK), BF16), s...  11.2 us
    unnamed x26, local copies, waits for them, and re-layouts  7.01 us
  transfers between devices with their start and end apart: 1, of which 1 were waited for; matrix products, arithmetic and copies ran while one was open for 1% of the time, Pallas kernels for 39%

profile of v1, /device:TPU:1, one launch (start us, length us, event | category | flops | bytes accessed | tf_op | source)
XLA Modules:
  0.0 196.1 jit_solution(257677910504677398)
XLA Ops:
  6.5 0.0 all-gather.2.cloned.1.call-start
  6.5 0.7 all-gather.2.cloned.1.call-update
  7.3 0.7 convert_element_type.10
  8.0 0.9 compare_reduce_fusion
  8.9 0.1 copy.20
  9.0 0.1 broadcast_in_dim.26
  9.1 0.5 multiply_sine_fusion
  9.7 0.0 copy-start.6
  9.7 0.2 concatenate.6.turn_ref
  9.9 0.0 copy-start.2
  10.0 0.9 copy-done.2
  10.9 0.0 copy-start.3
  10.9 0.9 copy-done.3
  11.8 0.0 copy-start.4
  11.8 0.9 copy-done.4
  12.8 0.0 copy-start.5
  12.8 0.9 copy-done.5
  13.7 0.9 copy-done.7
  14.7 0.9 copy-done.8
  15.6 0.7 copy-done.9
  16.2 0.7 copy-done.10
  16.9 11.2 %delta_local.1 = (bf16[4,144,256]{2,1,0:T(8,128)(2,1)S(1)}, f32[4,256,128]{2,1,0:T(8,128)S(1)}, bf16[4,256,128]{2,1,0:T(8,128)(2,1)S(1)}, bf16[512,256]{1,0:T(8,128)(2,1)S(1)}, bf16[2,256,256]{2,1,0:T(8,128)(2,1)S(1)}) custom-call(bf16[256,256]{1,0:T(8,128)(2,1)S(1)} %copy-done.7, bf16[256,256]{1,0:T(8,128)(2,1)S(1)} %copy-done.8, ...), custom_call_target="tpu_custom_call" | custom-call | flops 2000000000 | bytes 4000000 | tf_op jit(solution)/shard_map/delta_local/pallas_call | solution.py:462
  28.1 0.0 copy-done.6
  28.1 65.7 %scan_attend.1 = (bf16[4,128,128]{2,1,0:T(8,128)(2,1)S(1)}, bf16[256,512]{1,0:T(8,128)(2,1)S(1)}) custom-call(bf16[4,144,256]{2,1,0:T(8,128)(2,1)S(1)} %get-tuple-element.12.maps_ref, bf16[512,256]{1,0:T(8,128)(2,1)S(1)} %get-tuple-element.13.qrot_ref, bf16[2,256,256]{2,1,0:T(8,128)(2,1)S(1)} %get-tuple-element.14.kv_ref, ...), custom_call_target="tpu_custom_call" | custom-call | flops 2000000000 | bytes 100000000 | tf_op jit(solution)/shard_map/scan_attend/pallas_call | solution.py:479
  93.8 66.3 %all-gather.2.cloned.1.call-done = bf16[2048,2,512]{2,0,1:T(8,128)(2,1)} async-done(((bf16[32,2,512]{2,0,1:T(8,128)(2,1)}), bf16[2048,2,512]{2,0,1:T(8,128)(2,1)}) %all-gather.2.cloned.1.call-update) | async-done | bytes 4194320 | tf_op jit(solution)/shard_map/all_gather | solution.py:442
  160.0 2.8 %copy.24 = bf16[8,8,32,2,512]{4,2,3,1,0:T(8,128)(2,1)S(1)} copy(bf16[8,8,32,2,512]{4,2,1,0,3:T(8,128)(2,1)} %bitcast.12) | data formatting | bytes 8388608 | tf_op jit(solution)/shard_map/reshape | solution.py:443
  162.9 0.0 copy-start.11
  162.9 0.0 copy-done
  162.9 0.0 copy-done.1
  162.9 25.7 %project_sum.1 = f32[256,256]{1,0:T(8,128)S(1)} custom-call(bf16[4,128,128]{2,1,0:T(8,128)(2,1)S(1)} %get-tuple-element.15.state_ref, f32[4,256,128]{2,1,0:T(8,128)S(1)} %get-tuple-element.16.r0_ref, bf16[4,256,128]{2,1,0:T(8,128)(2,1)S(1)} %get-tuple-element.17.qe_ref, bf16[256,512]{1,0:T(8,128)(2,1)S(1)} %copy-done, f32[1,128]{1,0:T(1,128)S(1)} %bitcast.11, ...), custom_call_target="tpu_custom_call" | custom-call | tf_op jit(solution)/shard_map/project_sum/pallas_call | solution.py:506
  188.6 0.0 copy-done.11
  188.6 0.7 add_convert_fusion
  (16 shorter events, 0.1 us)
Async XLA Ops:
  6.5 153.5 %all-gather.2.cloned.1.call-start = ((), (), s32[]{:S(2)}) async-start(), calls=%async_computation | async-start | bytes 4259840 | tf_op jit(solution)/shard_map/all_gather | solution.py:442
  9.7 18.4 %copy-start.6 = (bf16[256,512]{1,0:T(8,128)(2,1)S(1)}, bf16[256,512]{1,0:T(8,128)(2,1)}, u32[]{:S(2)}) copy-start(bf16[256,512]{1,0:T(8,128)(2,1)} %gate_ref.2) | copy-start | bytes 786436
  9.9 1.0 copy-start.2
  10.9 0.9 copy-start.3
  11.8 0.9 copy-start.4
  12.8 0.9 copy-start.5
  13.7 0.9 copy-start.7
  14.7 0.9 copy-start.8
  15.6 0.7 copy-start.9
  16.2 0.7 copy-start.10
  160.0 2.8 %copy-start = (bf16[256,512]{1,0:T(8,128)(2,1)S(1)}, bf16[256,512]{1,0:T(8,128)(2,1)}, u32[]{:S(2)}) copy-start(bf16[256,512]{1,0:T(8,128)(2,1)} %gate_ref.3) | copy-start | bytes 786436
  160.0 2.8 %copy-start.1 = (f32[128]{0:T(128)S(1)}, f32[128]{0:T(128)}, u32[]{:S(2)}) copy-start(f32[128]{0:T(128)} %param.22) | copy-start | bytes 1540
  162.9 25.8 %copy-start.11 = (bf16[256,256]{1,0:T(8,128)(2,1)S(1)}, bf16[256,256]{1,0:T(8,128)(2,1)}, u32[]{:S(2)}) copy-start(bf16[256,256]{1,0:T(8,128)(2,1)} %param.15) | copy-start | bytes 393220
Sparse Core Ops, SparseCore 0:
  10.3 149.6 all-gather.1

commit v2 on v1

v2 whole, which is shorter than its diff:
```python
import jax
import jax.numpy as jnp
import numpy as np
from jax import lax
from jax.experimental import pallas as pl
from jax.experimental.pallas import tpu as pltpu
from jax.sharding import PartitionSpec as P

DK = 128
AH = 16
KVH = 2
HA = 256
BLK = 128
SPAN = 6
ROT = 64
TOK = 256
ZN = 16
YN = 4
GRP = 4
MAPR = 144
MESH = pl.DeviceIdType.MESH
F32 = jnp.float32
BF16 = jnp.bfloat16
ANY = pl.BlockSpec(memory_space=pl.ANY)
VMEM = pl.BlockSpec(memory_space=pltpu.VMEM)
MB = 1 << 20


def dot(a, b):
    return jnp.dot(a, b, preferred_element_type=F32)


def dot_nt(a, b):
    return lax.dot_general(a, b, (((1,), (1,)), ((), ())), preferred_element_type=F32)


def iota(shape, axis):
    return lax.broadcasted_iota(jnp.int32, shape, axis)


def base_inverse(lower):
    row = iota((TOK, 128), 0)
    lane = iota((TOK, 128), 1)
    left = jnp.where(row // 16 == lane // 16, lower[:, :128], 0.0)
    right = jnp.where(row // 16 == (lane + 128) // 16, lower[:, 128:], 0.0)
    folded = left + right
    for step in (64, 32, 16):
        folded = folded + pltpu.roll(folded, step, 1)
    low3 = folded.reshape(16, 16, 128)
    inv3 = jnp.where(row % 16 == lane % 16, 1.0, 0.0).astype(F32).reshape(16, 16, 128)
    for j in range(15):
        inv3 = inv3 - low3[:, :, j : j + 1] * inv3[:, j : j + 1, :]
    return inv3.reshape(TOK, 128)


def merge_blocks(lower, compact):
    r1 = iota((128, 128), 0)
    c1 = iota((128, 128), 1)
    halves = []
    for part in range(2):
        rows = slice(part * 128, part * 128 + 128)
        inv = jnp.where(r1 // 16 == c1 // 16, compact[rows], 0.0)
        low = lower[rows, rows]
        for size in (16, 32, 64):
            between = (r1 // (2 * size) == c1 // (2 * size)) & (r1 // size != c1 // size)
            off = jnp.where(between, low, 0.0)
            hi = inv.astype(BF16)
            inv = inv - dot(hi, dot(off.astype(BF16), hi).astype(BF16))
        halves.append(inv)
    inner = dot(lower[128:, :128].astype(BF16), halves[0].astype(BF16))
    cross = -dot(halves[1].astype(BF16), inner.astype(BF16))
    top = jnp.concatenate([halves[0], jnp.zeros((128, 128), F32)], 1)
    return jnp.concatenate([top, jnp.concatenate([cross, halves[1]], 1)], 0)


def gamma_rows(gamma):
    high = gamma.astype(BF16).astype(F32)
    middle = (gamma - high).astype(BF16).astype(F32)
    low = gamma - high - middle
    row = iota((16, gamma.shape[1]), 0)
    rows = jnp.where(row == 0, high, jnp.where(row == 1, middle, jnp.where(row == 2, low, 0.0)))
    return rows.astype(BF16)


def read_map(ref, index):
    tail = ref[index, DK:, :].astype(F32)
    gamma = tail[0:1] + tail[1:2] + tail[2:3]
    return gamma, ref[index, :DK, :].astype(F32)


def join(later, earlier):
    gl, xl = later
    ge, xe = earlier
    scaled = jnp.concatenate([xl[:, :DK] * ge[:, :DK], xl[:, DK:]], 1)
    return gl * ge, gl * xe + scaled - dot(xl[:, :DK].astype(BF16), xe.astype(BF16))


def apply_map(one, state):
    gamma, x = one
    return gamma[:, :DK] * state + x[:, DK:] - dot(x[:, :DK].astype(BF16), state.astype(BF16))


def write_map(ref, index, one):
    gamma, x = one
    ref[index, :DK, :] = x.astype(BF16)
    ref[index, DK:, :] = gamma_rows(gamma)


def mixer_kernel(
    w_hbm, dk_hbm, dq_hbm, dv_hbm, ak_hbm, av_hbm, aq_hbm, og_hbm, ag_hbm,
    wr_ref, ld_ref, pos_ref, list_ref, turn_ref, gain_ref,
    out_ref,
    wall, dk_ref, dq_ref, dv_ref, ak_ref, av_ref, aq_ref, og_ref, ag_ref,
    low_s, both_s, reads_s, r0_s, qe_s, qrot, own,
    maps, l1, l2, l3, pre, pregam, prefix, prefgam, csend, cgot, ssend, sgot,
    kvbuf, m_scr, l_scr, acc, mixed, attn, sbuf, rbuf,
    ins, s1, r1, s2, r2, s3, r3, sc, rc, s4, r4, kzs, kzr, kcs, kcr, wps, wpr, wms, wmr, wys, wyr, rss, rsr,
):
    c = lax.axis_index("ctx")
    mp = lax.axis_index("mp")
    y = c // ZN
    z = c % ZN
    zlo = z % GRP
    zhi = z // GRP
    core = mp % 2
    sibling = mp + 1 - 2 * core
    after = (c + 1) % (ZN * YN)
    before = (c + ZN * YN - 1) % (ZN * YN)
    z_up = (y * ZN + (z + 1) % ZN, mp)
    z_down = (y * ZN + (z + ZN - 1) % ZN, mp)

    def lo_peer(d):
        return (zlo + d) % GRP

    def lo_dev(d):
        return (y * ZN + zhi * GRP + lo_peer(d), mp)

    def hi_dev(d):
        return (y * ZN + ((zhi + d) % GRP) * GRP + zlo, mp)

    def y_dev(d):
        return (((y + d) % YN) * ZN + z, mp)

    def mp_dev(d):
        return (c, (mp + d) % 8)

    barrier = pltpu.get_barrier_semaphore()
    peers = [f(d) for f in (lo_dev, hi_dev, y_dev) for d in (1, 2, 3)] + [mp_dev(d) for d in range(1, 8)]
    peers += [(after, mp), (before, mp), z_up, z_down]
    for peer in peers:
        pl.semaphore_signal(barrier, inc=1, device_id=peer, device_id_type=MESH)

    moves = [
        (w_hbm, wall.at[y, z]),
        (dk_hbm, dk_ref),
        (dq_hbm, dq_ref),
        (ak_hbm, ak_ref),
        (av_hbm, av_ref),
        (dv_hbm, dv_ref),
        (aq_hbm, aq_ref),
        (ag_hbm, ag_ref),
        (og_hbm, og_ref),
    ]
    moves = [pltpu.make_async_copy(src, dst, ins.at[i]) for i, (src, dst) in enumerate(moves)]
    for move in moves:
        move.start()

    def remote(src, dst, send, recv, device):
        return pltpu.make_async_remote_copy(
            src_ref=src, dst_ref=dst, send_sem=send, recv_sem=recv, device_id=device, device_id_type=MESH
        )

    def c1(d):
        return remote(maps.at[lo_peer(d)], l1.at[zlo], s1.at[d - 1], r1.at[d - 1], lo_dev(d))

    def c2(d):
        return remote(l2.at[zhi], l2.at[zhi], s2.at[d - 1], r2.at[d - 1], hi_dev(d))

    def c3(d):
        return remote(l3.at[y], l3.at[y], s3.at[d - 1], r3.at[d - 1], y_dev(d))

    def cc(d):
        return remote(csend, cgot, sc.at[d - 1], rc, hi_dev(d))

    def c4(d):
        return remote(ssend.at[lo_peer(d)], sgot.at[zlo], s4.at[d - 1], r4.at[d - 1], lo_dev(d))

    def kz(s):
        src = own.at[core] if s == 1 else kvbuf.at[s - 2, core]
        return remote(src, kvbuf.at[s - 1, core], kzs.at[s - 1], kzr.at[s - 1], (after, mp))

    def kc(s):
        return remote(kvbuf.at[s - 1, core], kvbuf.at[s - 1, core], kcs.at[s - 1], kcr.at[s - 1], (c, sibling))

    def kv_step(s):
        kz(s).wait_recv()
        if s < SPAN:
            kz(s + 1).start()
        kc(s).start()

    def wz_up(k):
        block = wall.at[y, (z + ZN - k + 1) % ZN]
        return remote(block, block, wps.at[k - 1], wpr.at[k - 1], z_up)

    def wz_down(k):
        block = wall.at[y, (z + k - 1) % ZN]
        return remote(block, block, wms.at[k - 1], wmr.at[k - 1], z_down)

    def wy_send(zs):
        for d in (2, 1, 3):
            remote(wall.at[y, zs], wall.at[y, zs], wys.at[d - 1], wyr.at[d - 1], y_dev(d)).start()

    def wy_all(d):
        return remote(wall.at[y], wall.at[y], wys.at[d - 1], wyr.at[d - 1], y_dev(d))

    up_steps, down_steps = ZN // 2, ZN // 2 - 1

    def w_step(k):
        wz_up(k).wait_recv()
        if k < up_steps:
            wz_up(k + 1).start()
        if k <= down_steps:
            wz_down(k).wait_recv()
            if k < down_steps:
                wz_down(k + 1).start()
        wy_send((z + ZN - k) % ZN)
        if k <= down_steps:
            wy_send((z + k) % ZN)

    rr = iota((TOK, TOK), 0)
    cc2 = iota((TOK, TOK), 1)
    upto = rr >= cc2
    strict = rr > cc2
    diag = rr == cc2
    tri = jnp.where(rr <= cc2, 1.0, 0.0).astype(F32)
    exact = lax.Precision.HIGHEST
    g_rows = jnp.dot(ld_ref[...], tri, precision=exact, preferred_element_type=F32)
    g_cols = jnp.transpose(jnp.concatenate([g_rows, g_rows], 0))
    b_cols = jnp.transpose(jnp.concatenate([wr_ref[...], wr_ref[...]], 0))
    place = jnp.transpose(jnp.broadcast_to(pos_ref[...].astype(F32), (8, TOK)))[:, 0:1]
    angle = place * turn_ref[0:1, :]
    cosine = jnp.cos(angle)
    sine = jnp.sin(angle) * turn_ref[1:2, :]
    lane = iota((TOK, 128), 1)

    def rotate(x):
        swapped = jnp.where(lane < ROT // 2, pltpu.roll(x, 128 - ROT // 2, 1), pltpu.roll(x, ROT // 2, 1))
        return x * cosine + swapped * sine

    moves[1].wait()
    moves[2].wait()
    rk_cols = []
    rq_cols = []
    rk_rows = []
    for kh in range(2):
        cols = slice(kh * DK, kh * DK + DK)
        kb = dk_ref[:, cols]
        qb = dq_ref[:, cols]
        qf = qb.astype(F32)
        gram = dot_nt(kb, kb)
        cross = dot_nt(qb, kb)
        square = jnp.where(diag, gram, 0.0)
        rk_col = lax.rsqrt(jnp.sum(square, 1, keepdims=True) + 1e-06)
        rk_row = lax.rsqrt(jnp.sum(square, 0, keepdims=True) + 1e-06)
        rq_col = lax.rsqrt(jnp.sum(qf * qf, 1, keepdims=True) + 1e-06)
        rk_cols.append(rk_col)
        rk_rows.append(rk_row)
        rq_cols.append(rq_col)
        for h in (2 * kh, 2 * kh + 1):
            spread = g_cols[:, h : h + 1] - g_rows[h : h + 1]
            fade = jnp.where(upto, jnp.exp(jnp.where(upto, spread, 0.0)), 0.0)
            low_s[h] = jnp.where(strict, fade * gram, 0.0) * (b_cols[:, h : h + 1] * rk_col) * rk_row
            reads_s[h] = (fade * cross * rq_col * rk_row).astype(BF16)

    moves[0].wait()
    pl.semaphore_wait(barrier, len(peers))
    wz_up(1).start()
    wz_down(1).start()
    wy_send(z)

    moves[3].wait()
    moves[4].wait()
    pair = mp // 4
    keys = jnp.where(pair == 0, ak_ref[:, :HA], ak_ref[:, HA:])
    values = jnp.where(pair == 0, av_ref[:, :HA], av_ref[:, HA:])
    turned = rotate(keys[:, :128].astype(F32)).astype(BF16)
    for half in range(2):
        rows = slice(half * 128, half * 128 + 128)
        own[half, :128, :128] = turned[rows]
        own[half, :128, 128:] = keys[rows, 128:]
        own[half, 128:, :] = values[rows]
    kz(1).start()

    bases = [base_inverse(low_s[h]) for h in range(4)]
    w_step(1)
    inverses = [merge_blocks(low_s[h], bases[h]) for h in range(4)]
    w_step(2)
    moves[5].wait()
    for h in range(4):
        kb = dk_ref[:, (h // 2) * DK : (h // 2) * DK + DK]
        kt = jnp.transpose(kb.astype(F32)).astype(BF16)
        g_row = g_rows[h : h + 1]
        g_col = g_cols[:, h : h + 1]
        b_row = wr_ref[h : h + 1, :]
        u = dot((inverses[h] * b_row).astype(BF16), dv_ref[:, h * DK : h * DK + DK])
        w = dot((inverses[h] * (b_row * jnp.exp(g_row) * rk_rows[h // 2])).astype(BF16), kb)
        both = jnp.concatenate([w, u], 1)
        both_s[h] = both.astype(BF16)
        g_end = g_col[TOK - 1 : TOK]
        pushed = (both * (jnp.exp(g_end - g_col) * rk_cols[h // 2])).astype(BF16)
        maps[h, :DK, :] = dot(kt, pushed).astype(BF16)
        maps[h, DK:, :] = gamma_rows(jnp.broadcast_to(jnp.exp(g_end), (1, 2 * DK)))
    for d in (2, 1, 3):
        c1(d).start()
    l1[zlo] = maps[zlo]
    w_step(3)

    for h in range(4):
        cols = slice((h // 2) * DK, (h // 2) * DK + DK)
        seen = dot(reads_s[h], both_s[h])
        r0_s[h] = seen[:, DK:]
        qf = dq_ref[:, cols].astype(F32)
        qe_s[h] = (jnp.exp(g_cols[:, h : h + 1]) * rq_cols[h // 2] * qf - seen[:, :DK]).astype(BF16)
    moves[6].wait()
    for head in range(2):
        rows = slice(head * TOK, head * TOK + TOK)
        first = aq_ref[:, head * HA : head * HA + 128].astype(F32)
        qrot[rows, :128] = rotate(first).astype(BF16) * BF16(1.0 / 16)
        qrot[rows, 128:] = aq_ref[:, head * HA + 128 : head * HA + HA] * BF16(1.0 / 16)
    kv_step(1)
    w_step(4)

    entries = list_ref[...]
    row16 = iota((16, TOK), 0)
    candidate = (c - row16 // 2) * 2 + iota((16, TOK), 1) // BLK
    hit = jnp.zeros((16, TOK), F32)
    for e in range(entries.shape[1]):
        entry = jnp.where(row16 % 2 == 0, entries[0:1, e : e + 1], entries[1:2, e : e + 1])
        hit = jnp.where(candidate == entry, 1.0, hit)
    bias16 = jnp.where((hit > 0.5) & (candidate >= 0), 0.0, -1e30)

    def attend(s):
        first = s == 0
        qk = []
        for half in range(2):
            block = own[half, :128, :] if first else kvbuf[s - 1, half, :128, :]
            qk.append(dot_nt(qrot[...], block))
        score = jnp.concatenate(qk, 1)
        rows = bias16[2 * s : 2 * s + 2, :]
        bias = jnp.concatenate(
            [jnp.broadcast_to(rows[qb : qb + 1], (BLK, TOK)) for _ in range(2) for qb in range(2)], 0
        )
        score = score + bias
        if first:
            r = iota((2 * TOK, TOK), 0) % TOK
            score = jnp.where(iota((2 * TOK, TOK), 1) <= r, score, -1e30)
        top = jnp.max(score, 1, keepdims=True)
        if not first:
            old = m_scr[...]
            top = jnp.maximum(old, top)
            fade = jnp.exp(old - top)
        weights = jnp.exp(score - top)
        total = jnp.sum(weights, 1, keepdims=True)
        wb = weights.astype(BF16)
        part = None
        for half in range(2):
            block = own[half, 128:, :] if first else kvbuf[s - 1, half, 128:, :]
            term = dot(wb[:, half * 128 : half * 128 + 128], block)
            part = term if part is None else part + term
        m_scr[...] = top
        if first:
            l_scr[...] = total
            acc[...] = part
        else:
            l_scr[...] = l_scr[...] * fade + total
            acc[...] = acc[...] * fade + part

    attend(0)
    for d in (1, 2, 3):
        c1(d).wait_recv()
    run = read_map(l1, 0)
    for i in range(1, GRP):
        pre[i - 1] = run[1]
        pregam[i - 1] = run[0]
        run = join(read_map(l1, i), run)
    write_map(l2, zhi, run)
    for d in (1, 2, 3):

        @pl.when(zhi + d < GRP)
        def _():
            c2(d).start()

    kv_step(2)
    w_step(5)
    kc(1).wait_recv()
    attend(1)
    w_step(6)

    for d in (1, 2, 3):

        @pl.when(zhi >= d)
        def _():
            c2(d).wait_recv()

    for number in range(1, GRP):

        @pl.when(zhi == number)
        def _():
            run = read_map(l2, 0)
            for i in range(1, number):
                run = join(read_map(l2, i), run)
            prefgam[...] = run[0]
            prefix[...] = run[1]

    last = zhi == GRP - 1

    @pl.when(last)
    def _():
        total = join(read_map(l2, GRP - 1), (prefgam[...], prefix[...]))
        write_map(l3, y, total)
        for d in (2, 1, 3):
            c3(d).start()

    kv_step(3)
    w_step(7)
    kc(2).wait_recv()
    attend(2)

    @pl.when(last)
    def _():
        for d in (1, 2, 3):
            c3(d).wait_recv()
        state = jnp.zeros((DK, DK), F32)
        carry = state
        for i in range(YN - 1):
            state = apply_map(read_map(l3, i), state)
            carry = jnp.where(y == i + 1, state, carry)
        csend[...] = carry.astype(BF16)
        for d in (2, 1, 3):
            cc(d).start()

    kv_step(4)
    w_step(8)
    kc(3).wait_recv()

    @pl.when(jnp.logical_not(last))
    def _():
        attend(3)
        remote(csend, cgot, sc.at[0], rc, hi_dev(1)).wait_recv()

    @pl.when(last)
    def _():
        cgot[...] = csend[...]

    ssend[0] = cgot[...]

    @pl.when(zhi > 0)
    def _():
        ssend[0] = apply_map((prefgam[...], prefix[...]), cgot[...].astype(F32)).astype(BF16)

    carry = ssend[0].astype(F32)
    for i in range(1, GRP):
        ssend[i] = apply_map((pregam[i - 1], pre[i - 1]), carry).astype(BF16)
    for d in (2, 1, 3):
        c4(d).start()
    sgot[zlo] = ssend[zlo]

    @pl.when(last)
    def _():
        attend(3)

    kv_step(5)
    kc(4).wait_recv()
    attend(4)
    kv_step(6)
    kc(5).wait_recv()
    attend(5)
    kc(6).wait_recv()
    attend(6)
    moves[7].wait()
    for head in range(2):
        rows = slice(head * TOK, head * TOK + TOK)
        cols = slice(head * HA, head * HA + HA)
        gate = ag_ref[:, cols].astype(F32)
        read = acc[rows, :] / l_scr[rows, :]
        attn[:, cols] = (read / (1.0 + jnp.exp(-gate))).astype(BF16)

    moves[8].wait()
    for d in (1, 2, 3):
        c4(d).wait_recv()
    for h in range(4):
        cols = slice(h * DK, h * DK + DK)
        read = r0_s[h] + dot(qe_s[h], sgot[h])
        scale = lax.rsqrt(jnp.mean(read * read, 1, keepdims=True) + 1e-06)
        gate = og_ref[:, cols].astype(F32)
        silu = gate / (1.0 + jnp.exp(-gate))
        mixed[:, cols] = (read * scale * gain_ref[...] * silu).astype(BF16)

    for d in (1, 2, 3):
        wy_all(d).wait_recv()

    def copy(d):
        return remote(sbuf.at[d - 1], rbuf.at[d - 1], rss.at[d - 1], rsr.at[d - 1], mp_dev(d))

    def term(d):
        to = (mp + d) % 8
        half = pl.ds((to % 2) * 8, 8)
        first = wall[to // 2, half, 0].reshape(256, 512)
        second = wall[to // 2, half, 1].reshape(256, 512)
        return (dot_nt(mixed[...], first) + dot_nt(attn[...], second)).astype(BF16)

    order = (4, 3, 5, 2, 6, 1, 7)
    for d in order:
        sbuf[d - 1] = term(d)
        copy(d).start()
    total = term(0).astype(F32)
    for d in order:
        copy(d).wait_recv()
        total = total + rbuf[d - 1].astype(F32)
    out_ref[...] = total

    for d in (1, 2, 3):
        c1(d).wait_send()
        c4(d).wait_send()
        wy_all(d).wait_send()

        @pl.when(zhi + d < GRP)
        def _():
            c2(d).wait_send()

        @pl.when(last)
        def _():
            c3(d).wait_send()
            cc(d).wait_send()

    for s in range(1, SPAN + 1):
        kz(s).wait_send()
        kc(s).wait_send()
    for k in range(1, up_steps + 1):
        wz_up(k).wait_send()
        if k <= down_steps:
            wz_down(k).wait_send()
    for d in order:
        copy(d).wait_send()


def turn_table():
    table = np.zeros((8, 128), np.float32)
    freq = np.power(1e7, -2.0 * np.arange(ROT // 2) / ROT)
    table[0, : ROT // 2] = freq
    table[0, ROT // 2 : ROT] = freq
    table[1, : ROT // 2] = -1.0
    table[1, ROT // 2 : ROT] = 1.0
    return table


def per_device(
    residual,
    delta_query,
    delta_key,
    delta_value,
    write_strength,
    log_decay,
    output_gate,
    norm_gain,
    attn_query,
    attn_key,
    attn_value,
    attn_gate,
    positions,
    block_lists,
    out_weight,
):
    weight_rows = jnp.transpose(out_weight, (0, 2, 1))
    dma = pltpu.SemaphoreType.DMA
    summed = pl.pallas_call(
        mixer_kernel,
        out_shape=jax.ShapeDtypeStruct((TOK, 256), F32),
        in_specs=[ANY] * 9 + [VMEM] * 6,
        out_specs=VMEM,
        scratch_shapes=[
            pltpu.VMEM((YN, ZN, 2, 32, 512), BF16),
            pltpu.VMEM((TOK, 2 * DK), BF16),
            pltpu.VMEM((TOK, 2 * DK), BF16),
            pltpu.VMEM((TOK, 4 * DK), BF16),
            pltpu.VMEM((TOK, 2 * HA), BF16),
            pltpu.VMEM((TOK, 2 * HA), BF16),
            pltpu.VMEM((TOK, 2 * HA), BF16),
            pltpu.VMEM((TOK, 4 * DK), BF16),
            pltpu.VMEM((TOK, 2 * HA), BF16),
            pltpu.VMEM((4, TOK, TOK), F32),
            pltpu.VMEM((4, TOK, 2 * DK), BF16),
            pltpu.VMEM((4, TOK, TOK), BF16),
            pltpu.VMEM((4, TOK, DK), F32),
            pltpu.VMEM((4, TOK, DK), BF16),
            pltpu.VMEM((2 * TOK, HA), BF16),
            pltpu.VMEM((2, TOK, HA), BF16),
            pltpu.VMEM((GRP, MAPR, 2 * DK), BF16),
            pltpu.VMEM((GRP, MAPR, 2 * DK), BF16),
            pltpu.VMEM((GRP, MAPR, 2 * DK), BF16),
            pltpu.VMEM((YN, MAPR, 2 * DK), BF16),
            pltpu.VMEM((GRP - 1, DK, 2 * DK), F32),
            pltpu.VMEM((GRP - 1, 1, 2 * DK), F32),
            pltpu.VMEM((DK, 2 * DK), F32),
            pltpu.VMEM((1, 2 * DK), F32),
            pltpu.VMEM((DK, DK), BF16),
            pltpu.VMEM((DK, DK), BF16),
            pltpu.VMEM((GRP, DK, DK), BF16),
            pltpu.VMEM((GRP, DK, DK), BF16),
            pltpu.VMEM((SPAN, 2, TOK, HA), BF16),
            pltpu.VMEM((2 * TOK, 1), F32),
            pltpu.VMEM((2 * TOK, 1), F32),
            pltpu.VMEM((2 * TOK, HA), F32),
            pltpu.VMEM((TOK, 4 * DK), BF16),
            pltpu.VMEM((TOK, 2 * HA), BF16),
            pltpu.VMEM((7, TOK, 256), BF16),
            pltpu.VMEM((7, TOK, 256), BF16),
            dma((9,)),
        ]
        + [dma((3,))] * 6
        + [dma((3,)), dma]
        + [dma((3,))] * 2
        + [dma((SPAN,))] * 4
        + [dma((ZN // 2,))] * 4
        + [dma((3,))] * 2
        + [dma((7,))] * 2,
        compiler_params=pltpu.CompilerParams(
            vmem_limit_bytes=56 * MB, collective_id=1, has_side_effects=True
        ),
        name="mixer",
    )(
        weight_rows, delta_key, delta_query, delta_value, attn_key, attn_value, attn_query, output_gate, attn_gate,
        write_strength, log_decay, positions.reshape(1, TOK), block_lists, jnp.asarray(turn_table()), norm_gain.reshape(1, DK),
    )
    return (residual.astype(F32) + summed).astype(BF16)


def solution(mesh):
    return jax.shard_map(
        per_device,
        mesh=mesh,
        in_specs=(
            P("ctx", "mp"),
            P("ctx", "mp"),
            P("ctx", "mp"),
            P("ctx", "mp"),
            P("mp", "ctx"),
            P("mp", "ctx"),
            P("ctx", "mp"),
            P(),
            P("ctx", "mp"),
            P("ctx", None),
            P("ctx", None),
            P("ctx", "mp"),
            P("ctx"),
            P("ctx", None),
            P(None, "mp", "ctx"),
        ),
        out_specs=P("ctx", "mp"),
        check_vma=False,
    )
```

time: 197 us -> 103 us (0.52)
  waiting for transfers between devices: 67 us -> 0 us
  between operations: 13.6 us -> 0.02 us
  local copies, waits for them, and re-layouts: 10.3 us -> 0.01 us
  Pallas kernels: 103 us -> 101 us
    all_gather x1 -> x0, waiting for transfers between devices: 66.3 us -> none  [per_device(): weight_all = lax.all_gather(weight_rows, 'ctx', axis=0, tiled=True)]
    unnamed x26 -> x2, local copies, waits for them, and re-layouts: 7.01 us -> 0.01 us
    reshape x1 -> x0, local copies, waits for them, and re-layouts: 2.81 us -> none  [per_device(): weight_all = weight_all.reshape(8, 8, 32, 2, 512).transpose(0, 1, 3, 2, 4)]
    pallas_call x3 -> x1, Pallas kernels: 103 us -> 101 us  [per_device(): pl.pallas_call(mixer_kernel, out_shape=jax.ShapeDtypeStruct((TOK, 256), F...]
  transfers between devices with their start and end apart: 1 -> 0, of which waited for: 1 -> 0; matrix products, arithmetic and copies ran while one was open for 1% -> 0% of each run, Pallas kernels for 39% -> 0%
where the time goes in v2:
time: 103 us
  Pallas kernels  101 us (98%)
  other arithmetic  1.63 us (2%)
    pallas_call x1, Pallas kernels, per_device(): pl.pallas_call(mixer_kernel, out_shape=jax.ShapeDtypeStruct((TOK, 256), F...  101 us

profile of v2, /device:TPU:1, one launch (start us, length us, event | category | flops | bytes accessed | tf_op | source)
XLA Modules:
  0.0 102.7 jit_solution(8319704512678214946)
XLA Ops:
  0.0 0.0 copy-start
  0.0 101.1 %mixer.1 = f32[256,256]{1,0:T(8,128)} custom-call(bf16[2,32,512]{2,1,0:T(8,128)(2,1)} %bitcast.3, bf16[256,256]{1,0:T(8,128)(2,1)} %dk_hbm.1, bf16[256,256]{1,0:T(8,128)(2,1)} %dq_hbm.1, bf16[256,512]{1,0:T(8,128)(2,1)} %dv_hbm.1, bf16[256,512]{1,0:T(8,128)(2,1)} %ak_hbm.1, bf16[256,512]{1,0:T(8,128)(2,1)} %av_hbm.1, bf16[256,512]{1,0:T(8,128)(2,1)} %aq_hbm.1, ...), custom_call_target="tpu_custom_call" | custom-call | tf_op jit(solution)/shard_map/mixer/pallas_call | solution.py:576
  101.1 0.0 copy-done
  101.1 1.6 %add_convert_fusion = bf16[256,256]{1,0:T(8,128)(2,1)} fusion(f32[256,256]{1,0:T(8,128)} %mixer.1, bf16[256,256]{1,0:T(8,128)(2,1)S(1)} %copy-done), kind=kLoop, calls=%fused_computation | loop fusion | flops 196608 | bytes 524288 | tf_op jit(solution)/shard_map/convert_element_type | solution.py:635
Async XLA Ops:
  0.0 101.1 %copy-start = (bf16[256,256]{1,0:T(8,128)(2,1)S(1)}, bf16[256,256]{1,0:T(8,128)(2,1)}, u32[]{:S(2)}) copy-start(bf16[256,256]{1,0:T(8,128)(2,1)} %param.16) | copy-start | bytes 393220

commit v3 on v2

--- a/solution.py
+++ b/solution.py
@@ -18,6 +18,16 @@
 YN = 4
 GRP = 4
 MAPR = 144
+WROWS = 64
+QTR = 4
+QROWS = TOK // QTR
+GAPS = (
+    ("k2", "a0", "w1"),
+    ("w2", "w3", "k4"),
+    ("w4", "a1"),
+    ("w5", "w6", "k6", "w7", "a2"),
+    ("w8", "a3", "a4", "a5", "a6"),
+)
 MESH = pl.DeviceIdType.MESH
 F32 = jnp.float32
 BF16 = jnp.bfloat16
@@ -111,10 +121,11 @@
     wr_ref, ld_ref, pos_ref, list_ref, turn_ref, gain_ref,
     out_ref,
     wall, dk_ref, dq_ref, dv_ref, ak_ref, av_ref, aq_ref, og_ref, ag_ref,
-    low_s, both_s, reads_s, r0_s, qe_s, qrot, own,
+    low_s, rhs_s, kts_s, both_s, reads_s, r0_s, qe_s, qrot, own,
     maps, l1, l2, l3, pre, pregam, prefix, prefgam, csend, cgot, ssend, sgot,
-    kvbuf, m_scr, l_scr, acc, mixed, attn, sbuf, rbuf,
-    ins, s1, r1, s2, r2, s3, r3, sc, rc, s4, r4, kzs, kzr, kcs, kcr, wps, wpr, wms, wmr, wys, wyr, rss, rsr,
+    kvbuf, m_scr, l_scr, acc, mixed, attn, tosib, fromsib, sbuf, rbuf,
+    ins, s1, r1, s2, r2, s3, r3, sc, rc, s4, r4, kzs, kzr, kcs, kcr,
+    wps, wpr, wms, wmr, wys, wyr, ps, pr, rss, rsr,
 ):
     c = lax.axis_index("ctx")
     mp = lax.axis_index("mp")
@@ -124,8 +135,12 @@
     zhi = z // GRP
     core = mp % 2
     sibling = mp + 1 - 2 * core
-    after = (c + 1) % (ZN * YN)
-    before = (c + ZN * YN - 1) % (ZN * YN)
+    x = mp // 2
+    quarter = mp % QTR
+
+    def ctx_dev(d):
+        return ((c + ZN * YN + d) % (ZN * YN), mp)
+
     z_up = (y * ZN + (z + 1) % ZN, mp)
     z_down = (y * ZN + (z + ZN - 1) % ZN, mp)
 
@@ -146,7 +161,7 @@
 
     barrier = pltpu.get_barrier_semaphore()
     peers = [f(d) for f in (lo_dev, hi_dev, y_dev) for d in (1, 2, 3)] + [mp_dev(d) for d in range(1, 8)]
-    peers += [(after, mp), (before, mp), z_up, z_down]
+    peers += [ctx_dev(d) for d in (1, 2, -1, -2)] + [z_up, z_down]
     for peer in peers:
         pl.semaphore_signal(barrier, inc=1, device_id=peer, device_id_type=MESH)
 
@@ -186,43 +201,69 @@
         return remote(ssend.at[lo_peer(d)], sgot.at[zlo], s4.at[d - 1], r4.at[d - 1], lo_dev(d))
 
     def kz(s):
-        src = own.at[core] if s == 1 else kvbuf.at[s - 2, core]
-        return remote(src, kvbuf.at[s - 1, core], kzs.at[s - 1], kzr.at[s - 1], (after, mp))
-
-    def kc(s):
-        return remote(kvbuf.at[s - 1, core], kvbuf.at[s - 1, core], kcs.at[s - 1], kcr.at[s - 1], (c, sibling))
-
-    def kv_step(s):
+        odd = s % 2
+        src = own.at[quarter] if s <= 2 else kvbuf.at[s - 2 if odd else s - 3, quarter]
+        return remote(src, kvbuf.at[s - 1, quarter], kzs.at[s - 1], kzr.at[s - 1], ctx_dev(1 if odd else 2))
+
+    def kc(s, d):
+        block = kvbuf.at[s - 1, quarter]
+        mate = (c, (mp // QTR) * QTR + (quarter + d) % QTR)
+        return remote(block, block, kcs.at[s - 1, d - 1], kcr.at[s - 1, d - 1], mate)
+
+    def kv_stage(s):
         kz(s).wait_recv()
         if s < SPAN:
+            kz(s + 2).start()
             kz(s + 1).start()
-        kc(s).start()
-
-    def wz_up(k):
-        block = wall.at[y, (z + ZN - k + 1) % ZN]
-        return remote(block, block, wps.at[k - 1], wpr.at[k - 1], z_up)
-
-    def wz_down(k):
-        block = wall.at[y, (z + k - 1) % ZN]
-        return remote(block, block, wms.at[k - 1], wmr.at[k - 1], z_down)
+        for d in (2, 3, 1):
+            kc(s, d).start()
+        kz(s - 1).wait_recv()
+        for d in (2, 3, 1):
+            kc(s - 1, d).start()
+
+    def kv_ready(s):
+        for d in (1, 2, 3):
+            kc(s, d).wait_recv()
+
+    def ring(block, k, sems):
+        up = block((z + ZN - k + 1) % ZN)
+        down = block((z + k - 1) % ZN)
+        return (
+            lambda: remote(up, up, sems[0].at[k - 1], sems[1].at[k - 1], z_up),
+            lambda: remote(down, down, sems[2].at[k - 1], sems[3].at[k - 1], z_down),
+        )
+
+    up_steps, down_steps = ZN // 2, ZN // 2 - 1
+
+    def ring_b(k):
+        return ring(lambda zs: wall.at[y, zs], k, (wps, wpr, wms, wmr))
 
     def wy_send(zs):
         for d in (2, 1, 3):
-            remote(wall.at[y, zs], wall.at[y, zs], wys.at[d - 1], wyr.at[d - 1], y_dev(d)).start()
+            block = wall.at[y, zs]
+            remote(block, block, wys.at[d - 1], wyr.at[d - 1], y_dev(d)).start()
 
     def wy_all(d):
         return remote(wall.at[y], wall.at[y], wys.at[d - 1], wyr.at[d - 1], y_dev(d))
 
-    up_steps, down_steps = ZN // 2, ZN // 2 - 1
+    def step_ring(which, k):
+        up, down = which(k)
+        further = which(k + 1) if k < up_steps else None
+        up().wait_recv()
+        if k < up_steps:
+            further[0]().start()
+        if k <= down_steps:
+            down().wait_recv()
+            if k < down_steps:
+                further[1]().start()
+
+    def w_start():
+        for copy in ring_b(1):
+            copy().start()
+        wy_send(z)
 
     def w_step(k):
-        wz_up(k).wait_recv()
-        if k < up_steps:
-            wz_up(k + 1).start()
-        if k <= down_steps:
-            wz_down(k).wait_recv()
-            if k < down_steps:
-                wz_down(k + 1).start()
+        step_ring(ring_b, k)
         wy_send((z + ZN - k) % ZN)
         if k <= down_steps:
             wy_send((z + k) % ZN)
@@ -249,9 +290,7 @@
 
     moves[1].wait()
     moves[2].wait()
-    rk_cols = []
     rq_cols = []
-    rk_rows = []
     for kh in range(2):
         cols = slice(kh * DK, kh * DK + DK)
         kb = dk_ref[:, cols]
@@ -263,20 +302,19 @@
         rk_col = lax.rsqrt(jnp.sum(square, 1, keepdims=True) + 1e-06)
         rk_row = lax.rsqrt(jnp.sum(square, 0, keepdims=True) + 1e-06)
         rq_col = lax.rsqrt(jnp.sum(qf * qf, 1, keepdims=True) + 1e-06)
-        rk_cols.append(rk_col)
-        rk_rows.append(rk_row)
         rq_cols.append(rq_col)
+        kf = kb.astype(F32)
+        kt = jnp.transpose(kf)
         for h in (2 * kh, 2 * kh + 1):
+            g_row = g_rows[h : h + 1]
+            g_col = g_cols[:, h : h + 1]
+            b_col = b_cols[:, h : h + 1]
+            rhs_s[h, :, :DK] = (kf * (b_col * jnp.exp(g_col) * rk_col)).astype(BF16)
+            kts_s[h] = (kt * (jnp.exp(g_row[:, TOK - 1 :] - g_row) * rk_row)).astype(BF16)
             spread = g_cols[:, h : h + 1] - g_rows[h : h + 1]
             fade = jnp.where(upto, jnp.exp(jnp.where(upto, spread, 0.0)), 0.0)
             low_s[h] = jnp.where(strict, fade * gram, 0.0) * (b_cols[:, h : h + 1] * rk_col) * rk_row
             reads_s[h] = (fade * cross * rq_col * rk_row).astype(BF16)
-
-    moves[0].wait()
-    pl.semaphore_wait(barrier, len(peers))
-    wz_up(1).start()
-    wz_down(1).start()
-    wy_send(z)
 
     moves[3].wait()
     moves[4].wait()
@@ -284,37 +322,32 @@
     keys = jnp.where(pair == 0, ak_ref[:, :HA], ak_ref[:, HA:])
     values = jnp.where(pair == 0, av_ref[:, :HA], av_ref[:, HA:])
     turned = rotate(keys[:, :128].astype(F32)).astype(BF16)
-    for half in range(2):
-        rows = slice(half * 128, half * 128 + 128)
-        own[half, :128, :128] = turned[rows]
-        own[half, :128, 128:] = keys[rows, 128:]
-        own[half, 128:, :] = values[rows]
+    for q in range(QTR):
+        rows = slice(q * QROWS, q * QROWS + QROWS)
+        own[q, :QROWS, :128] = turned[rows]
+        own[q, :QROWS, 128:] = keys[rows, 128:]
+        own[q, QROWS:, :] = values[rows]
+
+    moves[0].wait()
+    pl.semaphore_wait(barrier, len(peers))
+    w_start()
+    kz(2).start()
     kz(1).start()
 
-    bases = [base_inverse(low_s[h]) for h in range(4)]
-    w_step(1)
-    inverses = [merge_blocks(low_s[h], bases[h]) for h in range(4)]
-    w_step(2)
     moves[5].wait()
     for h in range(4):
-        kb = dk_ref[:, (h // 2) * DK : (h // 2) * DK + DK]
-        kt = jnp.transpose(kb.astype(F32)).astype(BF16)
-        g_row = g_rows[h : h + 1]
-        g_col = g_cols[:, h : h + 1]
-        b_row = wr_ref[h : h + 1, :]
-        u = dot((inverses[h] * b_row).astype(BF16), dv_ref[:, h * DK : h * DK + DK])
-        w = dot((inverses[h] * (b_row * jnp.exp(g_row) * rk_rows[h // 2])).astype(BF16), kb)
-        both = jnp.concatenate([w, u], 1)
-        both_s[h] = both.astype(BF16)
-        g_end = g_col[TOK - 1 : TOK]
-        pushed = (both * (jnp.exp(g_end - g_col) * rk_cols[h // 2])).astype(BF16)
-        maps[h, :DK, :] = dot(kt, pushed).astype(BF16)
-        maps[h, DK:, :] = gamma_rows(jnp.broadcast_to(jnp.exp(g_end), (1, 2 * DK)))
+        values = dv_ref[:, h * DK : h * DK + DK].astype(F32)
+        rhs_s[h, :, DK:] = (values * b_cols[:, h : h + 1]).astype(BF16)
+    bases = [base_inverse(low_s[h]) for h in range(4)]
+    inverses = [merge_blocks(low_s[h], bases[h]) for h in range(4)]
+    for h in range(4):
+        both = dot(inverses[h].astype(BF16), rhs_s[h]).astype(BF16)
+        both_s[h] = both
+        maps[h, :DK, :] = dot(kts_s[h], both).astype(BF16)
+        maps[h, DK:, :] = gamma_rows(jnp.broadcast_to(jnp.exp(g_cols[TOK - 1 :, h : h + 1]), (1, 2 * DK)))
     for d in (2, 1, 3):
         c1(d).start()
     l1[zlo] = maps[zlo]
-    w_step(3)
-
     for h in range(4):
         cols = slice((h // 2) * DK, (h // 2) * DK + DK)
         seen = dot(reads_s[h], both_s[h])
@@ -327,9 +360,6 @@
         first = aq_ref[:, head * HA : head * HA + 128].astype(F32)
         qrot[rows, :128] = rotate(first).astype(BF16) * BF16(1.0 / 16)
         qrot[rows, 128:] = aq_ref[:, head * HA + 128 : head * HA + HA] * BF16(1.0 / 16)
-    kv_step(1)
-    w_step(4)
-
     entries = list_ref[...]
     row16 = iota((16, TOK), 0)
     candidate = (c - row16 // 2) * 2 + iota((16, TOK), 1) // BLK
@@ -341,11 +371,8 @@
 
     def attend(s):
         first = s == 0
-        qk = []
-        for half in range(2):
-            block = own[half, :128, :] if first else kvbuf[s - 1, half, :128, :]
-            qk.append(dot_nt(qrot[...], block))
-        score = jnp.concatenate(qk, 1)
+        packed = own[...] if first else kvbuf[s - 1]
+        score = dot_nt(qrot[...], packed[:, :QROWS].reshape(TOK, HA))
         rows = bias16[2 * s : 2 * s + 2, :]
         bias = jnp.concatenate(
             [jnp.broadcast_to(rows[qb : qb + 1], (BLK, TOK)) for _ in range(2) for qb in range(2)], 0
@@ -361,12 +388,7 @@
             fade = jnp.exp(old - top)
         weights = jnp.exp(score - top)
         total = jnp.sum(weights, 1, keepdims=True)
-        wb = weights.astype(BF16)
-        part = None
-        for half in range(2):
-            block = own[half, 128:, :] if first else kvbuf[s - 1, half, 128:, :]
-            term = dot(wb[:, half * 128 : half * 128 + 128], block)
-            part = term if part is None else part + term
+        part = dot(weights.astype(BF16), packed[:, QROWS:].reshape(TOK, HA))
         m_scr[...] = top
         if first:
             l_scr[...] = total
@@ -375,26 +397,34 @@
             l_scr[...] = l_scr[...] * fade + total
             acc[...] = acc[...] * fade + part
 
-    attend(0)
+    def fill(gap):
+        for item in GAPS[gap]:
+            kind, number = item[0], int(item[1])
+            if kind == "w":
+                w_step(number)
+            elif kind == "k":
+                kv_stage(number)
+            else:
+                if number:
+                    kv_ready(number)
+                attend(number)
+
+    fill(0)
     for d in (1, 2, 3):
         c1(d).wait_recv()
-    run = read_map(l1, 0)
-    for i in range(1, GRP):
-        pre[i - 1] = run[1]
-        pregam[i - 1] = run[0]
-        run = join(read_map(l1, i), run)
-    write_map(l2, zhi, run)
+    parts = [read_map(l1, i) for i in range(GRP)]
+    early = join(parts[1], parts[0])
+    write_map(l2, zhi, join(join(parts[3], parts[2]), early))
     for d in (1, 2, 3):
 
         @pl.when(zhi + d < GRP)
         def _():
             c2(d).start()
 
-    kv_step(2)
-    w_step(5)
-    kc(1).wait_recv()
-    attend(1)
-    w_step(6)
+    for i, one in enumerate((parts[0], early, join(parts[2], early))):
+        pregam[i] = one[0]
+        pre[i] = one[1]
+    fill(1)
 
     for d in (1, 2, 3):
 
@@ -402,50 +432,56 @@
         def _():
             c2(d).wait_recv()
 
-    for number in range(1, GRP):
-
-        @pl.when(zhi == number)
-        def _():
-            run = read_map(l2, 0)
-            for i in range(1, number):
-                run = join(read_map(l2, i), run)
-            prefgam[...] = run[0]
-            prefix[...] = run[1]
+    def put_prefix(one):
+        prefgam[...] = one[0]
+        prefix[...] = one[1]
+
+    @pl.when(zhi == 1)
+    def _():
+        put_prefix(read_map(l2, 0))
+
+    @pl.when(zhi == 2)
+    def _():
+        put_prefix(join(read_map(l2, 1), read_map(l2, 0)))
 
     last = zhi == GRP - 1
 
     @pl.when(last)
     def _():
-        total = join(read_map(l2, GRP - 1), (prefgam[...], prefix[...]))
-        write_map(l3, y, total)
+        parts = [read_map(l2, i) for i in range(GRP)]
+        early = join(parts[1], parts[0])
+        write_map(l3, y, join(join(parts[3], parts[2]), early))
         for d in (2, 1, 3):
             c3(d).start()
-
-    kv_step(3)
-    w_step(7)
-    kc(2).wait_recv()
-    attend(2)
+        put_prefix(join(parts[2], early))
+
+    fill(2)
 
     @pl.when(last)
     def _():
         for d in (1, 2, 3):
             c3(d).wait_recv()
-        state = jnp.zeros((DK, DK), F32)
-        carry = state
-        for i in range(YN - 1):
+        state = read_map(l3, 0)[1][:, DK:]
+        carry = jnp.where(y == 1, state, 0.0)
+        for i in range(1, YN - 1):
             state = apply_map(read_map(l3, i), state)
             carry = jnp.where(y == i + 1, state, carry)
         csend[...] = carry.astype(BF16)
         for d in (2, 1, 3):
             cc(d).start()
 
-    kv_step(4)
-    w_step(8)
-    kc(3).wait_recv()
+    @pl.when(zhi > 0)
+    def _():
+        ahead = (prefgam[...], prefix[...])
+        for i in range(GRP - 1):
+            one = join((pregam[i], pre[i]), ahead)
+            pregam[i] = one[0]
+            pre[i] = one[1]
+
+    fill(3)
 
     @pl.when(jnp.logical_not(last))
     def _():
-        attend(3)
         remote(csend, cgot, sc.at[0], rc, hi_dev(1)).wait_recv()
 
     @pl.when(last)
@@ -453,30 +489,18 @@
         cgot[...] = csend[...]
 
     ssend[0] = cgot[...]
+    carry = cgot[...].astype(F32)
 
     @pl.when(zhi > 0)
     def _():
-        ssend[0] = apply_map((prefgam[...], prefix[...]), cgot[...].astype(F32)).astype(BF16)
-
-    carry = ssend[0].astype(F32)
+        ssend[0] = apply_map((prefgam[...], prefix[...]), carry).astype(BF16)
+
     for i in range(1, GRP):
         ssend[i] = apply_map((pregam[i - 1], pre[i - 1]), carry).astype(BF16)
     for d in (2, 1, 3):
         c4(d).start()
     sgot[zlo] = ssend[zlo]
-
-    @pl.when(last)
-    def _():
-        attend(3)
-
-    kv_step(5)
-    kc(4).wait_recv()
-    attend(4)
-    kv_step(6)
-    kc(5).wait_recv()
-    attend(5)
-    kc(6).wait_recv()
-    attend(6)
+    fill(4)
     moves[7].wait()
     for head in range(2):
         rows = slice(head * TOK, head * TOK + TOK)
@@ -499,23 +523,34 @@
     for d in (1, 2, 3):
         wy_all(d).wait_recv()
 
-    def copy(d):
-        return remote(sbuf.at[d - 1], rbuf.at[d - 1], rss.at[d - 1], rsr.at[d - 1], mp_dev(d))
-
-    def term(d):
-        to = (mp + d) % 8
-        half = pl.ds((to % 2) * 8, 8)
-        first = wall[to // 2, half, 0].reshape(256, 512)
-        second = wall[to // 2, half, 1].reshape(256, 512)
-        return (dot_nt(mixed[...], first) + dot_nt(attn[...], second)).astype(BF16)
-
-    order = (4, 3, 5, 2, 6, 1, 7)
+    def x_copy(d):
+        peer = (c, ((x + d) % 4) * 2 + core)
+        return remote(sbuf.at[d - 1], rbuf.at[d - 1], rss.at[d - 1], rsr.at[d - 1], peer)
+
+    def sib_copy(d):
+        return remote(tosib.at[d], fromsib.at[d], ps.at[d], pr.at[d], (c, sibling))
+
+    def term(d, side):
+        to = ((x + d) % 4) * 2 + side
+        half = pl.ds(side * 8, 8)
+        first = wall[to // 2, half, :32].reshape(256, 512)
+        second = wall[to // 2, half, 32:].reshape(256, 512)
+        return dot_nt(mixed[...], first) + dot_nt(attn[...], second)
+
+    order = (2, 1, 3, 0)
     for d in order:
-        sbuf[d - 1] = term(d)
-        copy(d).start()
-    total = term(0).astype(F32)
-    for d in order:
-        copy(d).wait_recv()
+        tosib[d] = term(d, 1 - core).astype(BF16)
+        sib_copy(d).start()
+    for d in order[:3]:
+        mine = term(d, core)
+        sib_copy(d).wait_recv()
+        sbuf[d - 1] = (mine + fromsib[d].astype(F32)).astype(BF16)
+        x_copy(d).start()
+    total = term(0, core)
+    sib_copy(0).wait_recv()
+    total = total + fromsib[0].astype(F32)
+    for d in order[:3]:
+        x_copy(d).wait_recv()
         total = total + rbuf[d - 1].astype(F32)
     out_ref[...] = total
 
@@ -535,13 +570,17 @@
 
     for s in range(1, SPAN + 1):
         kz(s).wait_send()
-        kc(s).wait_send()
+        for d in (1, 2, 3):
+            kc(s, d).wait_send()
+    for d in (1, 2, 3):
+        x_copy(d).wait_send()
     for k in range(1, up_steps + 1):
-        wz_up(k).wait_send()
+        up, down = ring_b(k)
+        up().wait_send()
         if k <= down_steps:
-            wz_down(k).wait_send()
+            down().wait_send()
     for d in order:
-        copy(d).wait_send()
+        sib_copy(d).wait_send()
 
 
 def turn_table():
@@ -571,7 +610,7 @@
     block_lists,
     out_weight,
 ):
-    weight_rows = jnp.transpose(out_weight, (0, 2, 1))
+    weight_rows = jnp.transpose(out_weight, (0, 2, 1)).reshape(WROWS, 512)
     dma = pltpu.SemaphoreType.DMA
     summed = pl.pallas_call(
         mixer_kernel,
@@ -579,7 +618,7 @@
         in_specs=[ANY] * 9 + [VMEM] * 6,
         out_specs=VMEM,
         scratch_shapes=[
-            pltpu.VMEM((YN, ZN, 2, 32, 512), BF16),
+            pltpu.VMEM((YN, ZN, WROWS, 512), BF16),
             pltpu.VMEM((TOK, 2 * DK), BF16),
             pltpu.VMEM((TOK, 2 * DK), BF16),
             pltpu.VMEM((TOK, 4 * DK), BF16),
@@ -590,11 +629,13 @@
             pltpu.VMEM((TOK, 2 * HA), BF16),
             pltpu.VMEM((4, TOK, TOK), F32),
             pltpu.VMEM((4, TOK, 2 * DK), BF16),
+            pltpu.VMEM((4, DK, TOK), BF16),
+            pltpu.VMEM((4, TOK, 2 * DK), BF16),
             pltpu.VMEM((4, TOK, TOK), BF16),
             pltpu.VMEM((4, TOK, DK), F32),
             pltpu.VMEM((4, TOK, DK), BF16),
             pltpu.VMEM((2 * TOK, HA), BF16),
-            pltpu.VMEM((2, TOK, HA), BF16),
+            pltpu.VMEM((QTR, 2 * QROWS, HA), BF16),
             pltpu.VMEM((GRP, MAPR, 2 * DK), BF16),
             pltpu.VMEM((GRP, MAPR, 2 * DK), BF16),
             pltpu.VMEM((GRP, MAPR, 2 * DK), BF16),
@@ -607,23 +648,27 @@
             pltpu.VMEM((DK, DK), BF16),
             pltpu.VMEM((GRP, DK, DK), BF16),
             pltpu.VMEM((GRP, DK, DK), BF16),
-            pltpu.VMEM((SPAN, 2, TOK, HA), BF16),
+            pltpu.VMEM((SPAN, QTR, 2 * QROWS, HA), BF16),
             pltpu.VMEM((2 * TOK, 1), F32),
             pltpu.VMEM((2 * TOK, 1), F32),
             pltpu.VMEM((2 * TOK, HA), F32),
             pltpu.VMEM((TOK, 4 * DK), BF16),
             pltpu.VMEM((TOK, 2 * HA), BF16),
-            pltpu.VMEM((7, TOK, 256), BF16),
-            pltpu.VMEM((7, TOK, 256), BF16),
+            pltpu.VMEM((4, TOK, 256), BF16),
+            pltpu.VMEM((4, TOK, 256), BF16),
+            pltpu.VMEM((3, TOK, 256), BF16),
+            pltpu.VMEM((3, TOK, 256), BF16),
             dma((9,)),
         ]
         + [dma((3,))] * 6
         + [dma((3,)), dma]
         + [dma((3,))] * 2
-        + [dma((SPAN,))] * 4
+        + [dma((SPAN,))] * 2
+        + [dma((SPAN, 3))] * 2
         + [dma((ZN // 2,))] * 4
         + [dma((3,))] * 2
-        + [dma((7,))] * 2,
+        + [dma((4,))] * 2
+        + [dma((3,))] * 2,
         compiler_params=pltpu.CompilerParams(
             vmem_limit_bytes=56 * MB, collective_id=1, has_side_effects=True
         ),

time: 103 us -> 94.9 us (0.921)
  Pallas kernels: 101 us -> 93.1 us
    pallas_call x1, Pallas kernels: 101 us -> 93.1 us  [per_device(): pl.pallas_call(mixer_kernel, out_shape=jax.ShapeDtypeStruct((TOK, 256), F...]
where the time goes in v3:
time: 94.9 us; the launch traced here: 94.7 us
  Pallas kernels  93.1 us (98%)
  other arithmetic  1.63 us (2%)
    pallas_call x1, Pallas kernels, per_device(): pl.pallas_call(mixer_kernel, out_shape=jax.ShapeDtypeStruct((TOK, 256), F...  93.1 us

profile of v3, /device:TPU:1, one launch (start us, length us, event | category | flops | bytes accessed | tf_op | source)
XLA Modules:
  0.0 94.7 jit_solution(5963604740180272799)
XLA Ops:
  0.0 0.0 copy-start
  0.0 93.1 %mixer.1 = f32[256,256]{1,0:T(8,128)} custom-call(bf16[64,512]{1,0:T(8,128)(2,1)} %bitcast.5, bf16[256,256]{1,0:T(8,128)(2,1)} %dk_hbm.1, bf16[256,256]{1,0:T(8,128)(2,1)} %dq_hbm.1, bf16[256,512]{1,0:T(8,128)(2,1)} %dv_hbm.1, bf16[256,512]{1,0:T(8,128)(2,1)} %ak_hbm.1, bf16[256,512]{1,0:T(8,128)(2,1)} %av_hbm.1, bf16[256,512]{1,0:T(8,128)(2,1)} %aq_hbm.1, ...), custom_call_target="tpu_custom_call" | custom-call | tf_op jit(solution)/shard_map/mixer/pallas_call | solution.py:615
  93.1 0.0 copy-done
  93.1 1.6 %add_convert_fusion = bf16[256,256]{1,0:T(8,128)(2,1)} fusion(f32[256,256]{1,0:T(8,128)} %mixer.1, bf16[256,256]{1,0:T(8,128)(2,1)S(1)} %copy-done), kind=kLoop, calls=%fused_computation | loop fusion | flops 196608 | bytes 524288 | tf_op jit(solution)/shard_map/convert_element_type | solution.py:680
Async XLA Ops:
  0.0 93.1 %copy-start = (bf16[256,256]{1,0:T(8,128)(2,1)S(1)}, bf16[256,256]{1,0:T(8,128)(2,1)}, u32[]{:S(2)}) copy-start(bf16[256,256]{1,0:T(8,128)(2,1)} %param.16) | copy-start | bytes 393220

commit v4 on v3

--- a/solution.py
+++ b/solution.py
@@ -268,6 +268,10 @@
         if k <= down_steps:
             wy_send((z + k) % ZN)
 
+    moves[0].wait()
+    pl.semaphore_wait(barrier, len(peers))
+    w_start()
+
     rr = iota((TOK, TOK), 0)
     cc2 = iota((TOK, TOK), 1)
     upto = rr >= cc2
@@ -328,9 +332,6 @@
         own[q, :QROWS, 128:] = keys[rows, 128:]
         own[q, QROWS:, :] = values[rows]
 
-    moves[0].wait()
-    pl.semaphore_wait(barrier, len(peers))
-    w_start()
     kz(2).start()
     kz(1).start()
 

time: 94.9 us -> 96.6 us (1.018)
  Pallas kernels: 93.1 us -> 94.7 us
    pallas_call x1, Pallas kernels: 93.1 us -> 94.7 us  [per_device(): pl.pallas_call(mixer_kernel, out_shape=jax.ShapeDtypeStruct((TOK, 256), F...]
where the time goes in v4:
time: 96.6 us; the launch traced here: 96.4 us
  Pallas kernels  94.7 us (98%)
  other arithmetic  1.63 us (2%)
    pallas_call x1, Pallas kernels, per_device(): pl.pallas_call(mixer_kernel, out_shape=jax.ShapeDtypeStruct((TOK, 256), F...  94.7 us

profile of v4, /device:TPU:1, one launch (start us, length us, event | category | flops | bytes accessed | tf_op | source)
XLA Modules:
  0.0 96.4 jit_solution(3818102736333447751)
XLA Ops:
  0.0 0.0 copy-start
  0.0 94.7 %mixer.1 = f32[256,256]{1,0:T(8,128)} custom-call(bf16[64,512]{1,0:T(8,128)(2,1)} %bitcast.5, bf16[256,256]{1,0:T(8,128)(2,1)} %dk_hbm.1, bf16[256,256]{1,0:T(8,128)(2,1)} %dq_hbm.1, bf16[256,512]{1,0:T(8,128)(2,1)} %dv_hbm.1, bf16[256,512]{1,0:T(8,128)(2,1)} %ak_hbm.1, bf16[256,512]{1,0:T(8,128)(2,1)} %av_hbm.1, bf16[256,512]{1,0:T(8,128)(2,1)} %aq_hbm.1, ...), custom_call_target="tpu_custom_call" | custom-call | tf_op jit(solution)/shard_map/mixer/pallas_call | solution.py:616
  94.7 0.0 copy-done
  94.7 1.6 %add_convert_fusion = bf16[256,256]{1,0:T(8,128)(2,1)} fusion(f32[256,256]{1,0:T(8,128)} %mixer.1, bf16[256,256]{1,0:T(8,128)(2,1)S(1)} %copy-done), kind=kLoop, calls=%fused_computation | loop fusion | flops 196608 | bytes 524288 | tf_op jit(solution)/shard_map/convert_element_type | solution.py:681
Async XLA Ops:
  0.0 94.7 %copy-start = (bf16[256,256]{1,0:T(8,128)(2,1)S(1)}, bf16[256,256]{1,0:T(8,128)(2,1)}, u32[]{:S(2)}) copy-start(bf16[256,256]{1,0:T(8,128)(2,1)} %param.16) | copy-start | bytes 393220
